TPU v7x, 256 devices: a whole 4x4x8 slice. The times are simulated.
256 devices in a mesh: date: 8 (over y, core), parcel: 32 (over x, z).
Axes of the slice: x: 4, y: 4, z: 8, core: 2. Of those that a mesh axis runs over, the one named last changes fastest.
Arguments:
- tile_pixels: bfloat16 [32, 4096, 640], P('date', 'parcel'), may hold values from -12 to 12
- owner: int32 [2048, 1], replicated, may hold values from 0 to 31; in each aligned block of 64 rows (0 to 63, 64 to 127, ...) at most 4 rows name the same one
- pix_count: int32 [2048], replicated, may hold values from 1 to 64
- cloud: int32 [2048, 32], P(('parcel', 'date')), may hold values 0 or 1
- w_pix1: bfloat16 [10, 128], replicated, may hold values from -2 to 2
- w_pix2: bfloat16 [128, 128], replicated, may hold values from -0.5 to 0.5
- w_embed: bfloat16 [256, 1024], replicated, may hold values from -2 to 2
- norm_gain: bfloat16 [1024], replicated, may hold values from 0.5 to 1.5
- w_qkv: bfloat16 [1024, 3072], replicated, may hold values from -0.1875 to 0.1875
- w_out: bfloat16 [1024, 1024], replicated, may hold values from -0.1875 to 0.1875
- head_scale: float32 [16], replicated, may hold values from 2 to 30
- logit_scale: float32 [1], replicated, may hold values from 5 to 30
- pos_ids: int32 [2048], P(('parcel', 'date')), may hold values from 0 to 255
- neg_ids: int32 [2048, 128], P(('parcel', 'date')), may hold values from 0 to 255
Outputs:
- parcel_embedding: bfloat16 [2048, 1024], P(('parcel', 'date'))
- contrast_loss: float32 [2048], P(('parcel', 'date'))
Inputs may be any that keep to these rules, and one draw needn't show every extreme that they name: Among the 64 parcels of one parcel owner (aligned blocks), at most 4 share one tile owner; some owner reaches 4.
All inputs are finite; a program needn't handle non-finite values. No bound on the sum of `cloud` on one device may be relied on, other than what follows from the above.
Results may differ from a plain program's by a relative error of at most 0.007.
Values may be sent and summed in bfloat16 or wider, within the bound.
No kernel may reach another device: no remote copies, remote signals or barrier semaphores. Data moves between devices by JAX's collectives and lax.ppermute only.
A program may use at most 64 MiB of HBM per device.

v0:
```python
import jax
import jax.numpy as jnp
from jax import lax
from jax.sharding import PartitionSpec as P

PAR_DEV = 64


def slot_ranks(block_owner, tile_count):
    tiles = jnp.arange(tile_count, dtype=jnp.int32)
    onehot = (block_owner[..., None] == tiles).astype(jnp.int32)
    before = jnp.cumsum(onehot, axis=-2) - onehot
    return jnp.sum(before * onehot, axis=-1)


def pool_pixels(pixels, counts, w_pix1, w_pix2):
    channels = w_pix1.shape[0]
    row_count = pixels.shape[0]
    pix_width = pixels.shape[1] // channels
    flattened = pixels.reshape(row_count * pix_width, channels)
    hidden_one = jax.nn.relu(jnp.dot(flattened, w_pix1, preferred_element_type=jnp.float32)).astype(
        jnp.bfloat16
    )
    hidden_two = jax.nn.relu(jnp.dot(hidden_one, w_pix2, preferred_element_type=jnp.float32))
    hidden_two = hidden_two.reshape(row_count, pix_width, -1)
    valid_mask = (jnp.arange(pix_width, dtype=jnp.int32)[None, :] < counts[:, None]).astype(
        jnp.float32
    )
    number = jnp.maximum(counts, 1).astype(jnp.float32)[:, None]
    center = jnp.sum(hidden_two * valid_mask[:, :, None], axis=1) / number
    spread = (
        jnp.sum(valid_mask[:, :, None] * (hidden_two - center[:, None, :]) ** 2, axis=1) / number
    )
    deviation = jnp.sqrt(jnp.maximum(spread, 0.01))
    return jnp.concatenate([center, deviation], axis=-1).astype(jnp.bfloat16)


def date_code(date_total, model_width):
    steps_t = jnp.arange(date_total, dtype=jnp.float32)[:, None]
    pair_index = jnp.arange(model_width // 2, dtype=jnp.float32)[None, :]
    angles = steps_t * jnp.exp(-2.0 * pair_index / model_width * jnp.log(10000.0))
    return jnp.stack([jnp.sin(angles), jnp.cos(angles)], axis=-1).reshape(date_total, model_width)


def unit_rows(vectors):
    return vectors * lax.rsqrt(jnp.sum(vectors * vectors, axis=-1, keepdims=True) + 1e-06)


def attend(tokens, cloudy, norm_gain, w_qkv, w_out, head_scale):
    date_total, parcels, model_width = tokens.shape
    head_count = head_scale.shape[0]
    date_state = tokens.astype(jnp.float32) + date_code(date_total, model_width)[:, None, :]
    center = jnp.mean(date_state, axis=-1, keepdims=True)
    spread = jnp.mean((date_state - center) ** 2, axis=-1, keepdims=True)
    normed = (
        (date_state - center) * lax.rsqrt(spread + 1e-05) * norm_gain.astype(jnp.float32)
    ).astype(jnp.bfloat16)
    packed = jnp.dot(normed.reshape(-1, model_width), w_qkv, preferred_element_type=jnp.float32)
    packed = packed.reshape(date_total, parcels, 3, head_count, model_width // head_count)
    queries = unit_rows(packed[:, :, 0])
    key_unit = unit_rows(packed[:, :, 1])
    values = packed[:, :, 2]
    scores = jnp.einsum("qphd,kphd->phqk", queries, key_unit) * head_scale[None, :, None, None]
    clear_dates = cloudy == 0
    diagonal_mask = jnp.arange(date_total)[:, None] == jnp.arange(date_total)[None, :]
    allowed = clear_dates[:, None, :] | diagonal_mask[None, :, :]
    scores = jnp.where(allowed[:, None, :, :], scores, -1000000000.0)
    weights = jax.nn.softmax(scores, axis=-1)
    mixed_heads = (
        jnp.einsum("phqk,kphd->qphd", weights, values).reshape(-1, model_width).astype(jnp.bfloat16)
    )
    update = jnp.dot(mixed_heads, w_out, preferred_element_type=jnp.float32).reshape(
        date_total, parcels, model_width
    )
    return jnp.mean(date_state + update, axis=0).astype(jnp.bfloat16)


def contrast(similarity, pos_ids, neg_ids, logit_scale):
    positive = jnp.take_along_axis(similarity, pos_ids[:, None], axis=1) * logit_scale[0]
    negative = jnp.take_along_axis(similarity, neg_ids, axis=1) * logit_scale[0]
    logits = jnp.concatenate([positive, negative], axis=1)
    return jax.nn.logsumexp(logits, axis=1) - positive[:, 0]


def per_device(
    tile_pixels,
    owner,
    pix_count,
    cloud,
    w_pix1,
    w_pix2,
    w_embed,
    norm_gain,
    w_qkv,
    w_out,
    head_scale,
    logit_scale,
    pos_ids,
    neg_ids,
):
    parcel_devices = lax.axis_size("parcel")
    capacity = tile_pixels.shape[1] // parcel_devices
    model_width = w_out.shape[0]
    my_block = lax.axis_index("parcel")
    block_start = my_block * PAR_DEV
    my_owner = lax.dynamic_slice_in_dim(owner[:, 0], block_start, PAR_DEV)
    my_counts = lax.dynamic_slice_in_dim(pix_count, block_start, PAR_DEV)
    my_rows = my_owner * capacity + slot_ranks(my_owner, parcel_devices)
    picked = jnp.take(
        lax.all_to_all(tile_pixels, "parcel", split_axis=1, concat_axis=1, tiled=True),
        my_rows,
        axis=1,
    )

    def encode_date(one_date):
        return pool_pixels(one_date, my_counts, w_pix1, w_pix2)

    pooled = lax.map(encode_date, picked)
    date_count = pooled.shape[0]
    row_count = pooled.shape[1]
    flat_rows = pooled.reshape(-1, pooled.shape[-1])
    encoded_rows = jnp.dot(flat_rows, w_embed, preferred_element_type=jnp.float32).astype(
        jnp.bfloat16
    )
    moving = encoded_rows.reshape(date_count, row_count, model_width)
    tokens = lax.all_to_all(moving, "date", split_axis=1, concat_axis=0, tiled=True)
    embedding = attend(tokens, cloud, norm_gain, w_qkv, w_out, head_scale)
    anchors = unit_rows(embedding.astype(jnp.float32))
    others = unit_rows(lax.all_gather(embedding, "parcel", axis=0, tiled=True).astype(jnp.float32))
    score_block = jnp.einsum("ad,bd->ab", anchors, others, precision=lax.Precision.HIGHEST)
    return (embedding, contrast(score_block, pos_ids, neg_ids, logit_scale))


def solution(mesh):
    in_specs = (
        P("date", "parcel", None),
        P(),
        P(),
        P(("parcel", "date"), None),
        P(),
        P(),
        P(),
        P(),
        P(),
        P(),
        P(),
        P(),
        P(("parcel", "date")),
        P(("parcel", "date"), None),
    )
    out_specs = (P(("parcel", "date"), None), P(("parcel", "date")))
    return jax.shard_map(
        per_device, mesh=mesh, in_specs=in_specs, out_specs=out_specs, check_vma=False
    )
```

profile of v0, /device:TPU:32, one launch (start us, length us, event | category | flops | bytes accessed | tf_op | source)
XLA Modules:
  0.0 173.5 jit_solution(8192680852443072894)
XLA Ops:
  0.7 2.6 %copy.35 = bf16[4,128,640]{2,0,1:T(4,128)(2,1)} copy(bf16[4,128,640]{2,1,0:T(8,128)(2,1)} %param.16) | data formatting | bytes 1310720 | tf_op args[0]
  3.2 11.3 %all-to-all-start = ((bf16[4,128,640]{2,0,1:T(4,128)(2,1)}), bf16[4,128,640]{2,0,1:T(4,128)(2,1)S(1)}, u32[]{:S(2)}, u32[]{:S(2)}) async-start(bf16[4,128,640]{2,0,1:T(4,128)(2,1)} %copy.35), calls=%async_computation | async-start | bytes 1310720 | tf_op jit(solution)/shard_map/all_to_all | solution.py:110
  15.5 1.3 dynamic_slice.11
  19.3 15.6 %all-to-all-done = bf16[4,128,640]{2,0,1:T(4,128)(2,1)S(1)} async-done(((bf16[4,128,640]{2,0,1:T(4,128)(2,1)}), bf16[4,128,640]{2,0,1:T(4,128)(2,1)S(1)}, u32[]{:S(2)}, u32[]{:S(2)}) %all-to-all-start) | async-done | bytes 655392 | tf_op jit(solution)/shard_map/all_to_all | solution.py:110
  34.8 0.9 gather_fusion
  36.0 0.8 copy.36
  36.8 36.2 %while.10 = (s32[]{:T(128)}, bf16[4,64,256]{2,1,0:T(8,128)(2,1)S(1)}, bf16[4,64,640]{2,1,0:T(8,128)(2,1)}, bf16[10,128]{1,0:T(8,128)(2,1)}, bf16[128,128]{1,0:T(8,128)(2,1)S(1)}, /*index=5*/s32[64]{0:T(128)}, s32[]{:T(128)}) while((s32[]{:T(128)}, bf16[4,64,256]{2,1,0:T(8,128)(2,1)S(1)}, bf16[4,64,640]{2,1,0:T(8,128)(2,1)}, ...), condition=%wide.region_5.6_spmd, body=%wide.region_2.5_spmd.sunk | while | flops 149520512 | bytes 4985713 | solution.py:118
  36.8 0.9 constant_dynamic-slice_fusion.3
  37.7 2.3 %reshape.394 = bf16[4096,10]{1,0:T(8,128)(2,1)S(1)} reshape(bf16[1,64,640]{2,1,0:T(8,128)(2,1)S(1)} %constant_dynamic-slice_fusion.3) | data formatting | bytes 163840 | tf_op jit(solution)/shard_map/while/body/eval_jaxpr/reshape | solution.py:20
  40.0 0.8 fusion.76
  40.8 2.8 %multiply_reduce_fusion.7 = (f32[64,128]{1,0:T(8,128)S(1)}, f32[4096,128]{1,0:T(8,128)}) fusion(f32[64,64]{1,0:T(8,128)S(1)} %fusion.76, bf16[128,128]{1,0:T(8,128)(2,1)S(1)} %get-tuple-element.144, bf16[4096,10]{1,0:T(8,128)(2,1)S(1)} %reshape.394, bf16[10,128]{1,0:T(8,128)(2,1)} %get-tuple-element.143), kind=kOutput, calls=%fused_computation.7.clone.1 | convolution fusion | flops 147316736 | bytes 2263552 | tf_op jit(solution)/shard_map/while/body/eval_jaxpr/dot_general | solution.py:24
  43.7 1.9 %multiply_reduce_fusion.8 = f32[64,128]{1,0:T(8,128)S(1)} fusion(f32[64,128]{1,0:T(8,128)S(1)} %get-tuple-element.123, f32[64,64]{1,0:T(8,128)S(1)} %fusion.76, f32[4096,128]{1,0:T(8,128)} %get-tuple-element.124), kind=kLoop, calls=%fused_computation.6.clone.1 | loop fusion | flops 2088960 | bytes 2179072 | tf_op jit(solution)/shard_map/while/body/eval_jaxpr/reduce_sum | solution.py:32
  45.8 0.9 constant_dynamic-slice_fusion.3
  46.7 2.3 %reshape.394 = bf16[4096,10]{1,0:T(8,128)(2,1)S(1)} reshape(bf16[1,64,640]{2,1,0:T(8,128)(2,1)S(1)} %constant_dynamic-slice_fusion.3) | data formatting | bytes 163840 | tf_op jit(solution)/shard_map/while/body/eval_jaxpr/reshape | solution.py:20
  49.0 0.8 fusion.76
  49.9 2.8 %multiply_reduce_fusion.7 = (f32[64,128]{1,0:T(8,128)S(1)}, f32[4096,128]{1,0:T(8,128)}) fusion(f32[64,64]{1,0:T(8,128)S(1)} %fusion.76, bf16[128,128]{1,0:T(8,128)(2,1)S(1)} %get-tuple-element.144, bf16[4096,10]{1,0:T(8,128)(2,1)S(1)} %reshape.394, bf16[10,128]{1,0:T(8,128)(2,1)} %get-tuple-element.143), kind=kOutput, calls=%fused_computation.7.clone.1 | convolution fusion | flops 147316736 | bytes 2263552 | tf_op jit(solution)/shard_map/while/body/eval_jaxpr/dot_general | solution.py:24
  52.8 1.9 %multiply_reduce_fusion.8 = f32[64,128]{1,0:T(8,128)S(1)} fusion(f32[64,128]{1,0:T(8,128)S(1)} %get-tuple-element.123, f32[64,64]{1,0:T(8,128)S(1)} %fusion.76, f32[4096,128]{1,0:T(8,128)} %get-tuple-element.124), kind=kLoop, calls=%fused_computation.6.clone.1 | loop fusion | flops 2088960 | bytes 2179072 | tf_op jit(solution)/shard_map/while/body/eval_jaxpr/reduce_sum | solution.py:32
  54.9 0.9 constant_dynamic-slice_fusion.3
  55.8 2.3 %reshape.394 = bf16[4096,10]{1,0:T(8,128)(2,1)S(1)} reshape(bf16[1,64,640]{2,1,0:T(8,128)(2,1)S(1)} %constant_dynamic-slice_fusion.3) | data formatting | bytes 163840 | tf_op jit(solution)/shard_map/while/body/eval_jaxpr/reshape | solution.py:20
  58.1 0.8 fusion.76
  58.9 2.8 %multiply_reduce_fusion.7 = (f32[64,128]{1,0:T(8,128)S(1)}, f32[4096,128]{1,0:T(8,128)}) fusion(f32[64,64]{1,0:T(8,128)S(1)} %fusion.76, bf16[128,128]{1,0:T(8,128)(2,1)S(1)} %get-tuple-element.144, bf16[4096,10]{1,0:T(8,128)(2,1)S(1)} %reshape.394, bf16[10,128]{1,0:T(8,128)(2,1)} %get-tuple-element.143), kind=kOutput, calls=%fused_computation.7.clone.1 | convolution fusion | flops 147316736 | bytes 2263552 | tf_op jit(solution)/shard_map/while/body/eval_jaxpr/dot_general | solution.py:24
  61.8 1.9 %multiply_reduce_fusion.8 = f32[64,128]{1,0:T(8,128)S(1)} fusion(f32[64,128]{1,0:T(8,128)S(1)} %get-tuple-element.123, f32[64,64]{1,0:T(8,128)S(1)} %fusion.76, f32[4096,128]{1,0:T(8,128)} %get-tuple-element.124), kind=kLoop, calls=%fused_computation.6.clone.1 | loop fusion | flops 2088960 | bytes 2179072 | tf_op jit(solution)/shard_map/while/body/eval_jaxpr/reduce_sum | solution.py:32
  63.9 0.9 constant_dynamic-slice_fusion.3
  64.8 2.3 %reshape.394 = bf16[4096,10]{1,0:T(8,128)(2,1)S(1)} reshape(bf16[1,64,640]{2,1,0:T(8,128)(2,1)S(1)} %constant_dynamic-slice_fusion.3) | data formatting | bytes 163840 | tf_op jit(solution)/shard_map/while/body/eval_jaxpr/reshape | solution.py:20
  67.1 0.8 fusion.76
  68.0 2.8 %multiply_reduce_fusion.7 = (f32[64,128]{1,0:T(8,128)S(1)}, f32[4096,128]{1,0:T(8,128)}) fusion(f32[64,64]{1,0:T(8,128)S(1)} %fusion.76, bf16[128,128]{1,0:T(8,128)(2,1)S(1)} %get-tuple-element.144, bf16[4096,10]{1,0:T(8,128)(2,1)S(1)} %reshape.394, bf16[10,128]{1,0:T(8,128)(2,1)} %get-tuple-element.143), kind=kOutput, calls=%fused_computation.7.clone.1 | convolution fusion | flops 147316736 | bytes 2263552 | tf_op jit(solution)/shard_map/while/body/eval_jaxpr/dot_general | solution.py:24
  70.9 1.9 %multiply_reduce_fusion.8 = f32[64,128]{1,0:T(8,128)S(1)} fusion(f32[64,128]{1,0:T(8,128)S(1)} %get-tuple-element.123, f32[64,64]{1,0:T(8,128)S(1)} %fusion.76, f32[4096,128]{1,0:T(8,128)} %get-tuple-element.124), kind=kLoop, calls=%fused_computation.6.clone.1 | loop fusion | flops 2088960 | bytes 2179072 | tf_op jit(solution)/shard_map/while/body/eval_jaxpr/reduce_sum | solution.py:32
  72.9 1.3 convolution_convert_fusion
  74.3 1.2 copy.37
  75.5 4.5 %all-to-all-start.1 = ((bf16[4,64,1024]{2,0,1:T(4,128)(2,1)}), bf16[4,64,1024]{2,0,1:T(4,128)(2,1)S(1)}, u32[]{:S(2)}, u32[]{:S(2)}) async-start(bf16[4,64,1024]{2,0,1:T(4,128)(2,1)} %copy.37), calls=%async_computation.1 | async-start | bytes 1048576 | tf_op jit(solution)/shard_map/all_to_all | solution.py:126
  80.2 2.8 %add.120 = f32[8,4,1024]{1,0,2:T(8,128)} reshape(f32[32,512,2]{0,2,1:T(2,128)S(1)} %copy.39) | data formatting | bytes 262144 | tf_op jit(solution)/shard_map/add | solution.py:52
  83.0 2.9 %copy.42 = f32[8,4,1024]{2,1,0:T(4,128)S(1)} copy(f32[8,4,1024]{1,0,2:T(8,128)} %add.120) | data formatting | bytes 262144 | tf_op jit(solution)/shard_map/add | solution.py:52
  85.9 8.7 %copy.43 = bf16[1024,3072]{0,1:T(8,128)(2,1)} copy(bf16[1024,3072]{1,0:T(8,128)(2,1)} %param.24) | data formatting | bytes 12582912 | tf_op args[8]
  95.7 0.8 fusion.41
  96.5 0.8 multiply_reduce_fusion.4
  97.4 0.8 multiply_convert_fusion
  98.1 5.6 %fusion.59 = f32[32,8,3,16,64]{4,1,3,2,0:T(8,128)S(1)} fusion(bf16[32,8,1024,1,1]{2,1,4,3,0:T(8,128)(2,1)S(1)} %bitcast.122, bf16[3,16,64,1024,1]{3,2,1,0,4:T(8,128)(2,1)} %bitcast.118), kind=kOutput, calls=%fused_computation.107 | convolution fusion | flops 1610612736 | bytes 9961472 | tf_op jit(solution)/shard_map/dot_general | solution.py:58
  103.7 1.2 multiply_reduce_fusion.3
  105.2 1.6 fusion.13
  106.8 2.6 %fusion.15 = (f32[8,16,32]{2,1,0:T(8,128)S(1)}, f32[8,16,32,32]{2,3,1,0:T(8,128)S(1)}) fusion(f32[16]{0:T(128)S(1)} %copy-done.9, pred[8,32,32]{1,2,0:T(8,128)(4,1)S(1)} %broadcast_or_fusion, bf16[32,8,16,64]{3,1,2,0:T(8,128)(2,1)S(1)} %get-tuple-element.74, bf16[32,8,16,64]{3,1,2,0:T(8,128)(2,1)S(1)} %get-tuple-element.73), kind=kOutput, calls=%fused_computation.36 | convolution fusion | flops 17166336 | bytes 1597504 | tf_op jit(solution)/shard_map/qphd,kphd->phqk/dot_general | solution.py:63
  109.3 0.8 fusion.16
  110.1 1.7 fusion.22
  111.9 1.4 copy.48
  113.3 1.9 %convert_element_type.102 = bf16[32,8,1024]{2,1,0:T(8,128)(2,1)S(1)} reshape(bf16[32,8,16,64]{3,2,1,0:T(8,128)(2,1)} %copy.48) | data formatting | bytes 1048576 | tf_op jit(solution)/shard_map/convert_element_type | solution.py:70
  115.6 1.5 fusion.30
  117.2 46.7 %all_gather.3 = bf16[256,1024]{1,0:T(8,128)(2,1)S(1)} all-gather(bf16[8,1024]{1,0:T(8,128)(2,1)S(1)} %get-tuple-element.68), channel_id=1, replica_groups=mesh['date'=8,'parcel'=32] {'parcel'}, dimensions={0}, use_global_device_ids=true | all-gather | bytes 540672 | tf_op jit(solution)/shard_map/all_gather | solution.py:129
  164.1 1.0 fusion.34
  165.1 6.8 %gather_fusion.2 = f32[1024]{0:T(1024)S(1)} fusion(f32[8,256]{1,0:T(8,128)S(1)} %fusion.34, s32[1024]{0:T(1024)S(1)} %fusion.51), kind=kCustom, calls=%fused_computation.2 | custom fusion | bytes 16384 | tf_op jit(solution)/shard_map/jit(take_along_axis)/gather | solution.py:80
  (86 shorter events, 7.5 us)
Async XLA Ops:
  0.6 114.9 %copy-start = (bf16[1024,1024]{1,0:T(8,128)(2,1)S(1)}, bf16[1024,1024]{1,0:T(8,128)(2,1)}, u32[]{:S(2)}) copy-start(bf16[1024,1024]{1,0:T(8,128)(2,1)} %param.25) | copy-start | bytes 6291460
  0.6 14.8 %copy-start.10 = (s32[8]{0:T(128)S(1)}, s32[8]{0:T(128)}, u32[]{:S(2)}) copy-start(s32[8]{0:T(128)} %param.28) | copy-start | bytes 100
  0.7 18.0 %copy-start.7 = (s32[8,32]{1,0:T(8,128)S(1)}, s32[8,32]{1,0:T(8,128)}, u32[]{:S(2)}) copy-start(s32[8,32]{1,0:T(8,128)} %param.19) | copy-start | bytes 3076
  3.2 33.5 %copy-start.1 = (bf16[128,128]{1,0:T(8,128)(2,1)S(1)}, bf16[128,128]{1,0:T(8,128)(2,1)}, u32[]{:S(2)}) copy-start(bf16[128,128]{1,0:T(8,128)(2,1)} %param.21) | copy-start | bytes 98308
  3.2 31.6 %all-to-all-start = ((bf16[4,128,640]{2,0,1:T(4,128)(2,1)}), bf16[4,128,640]{2,0,1:T(4,128)(2,1)S(1)}, u32[]{:S(2)}, u32[]{:S(2)}) async-start(bf16[4,128,640]{2,0,1:T(4,128)(2,1)} %copy.35), calls=%async_computation | async-start | bytes 1310720 | tf_op jit(solution)/shard_map/all_to_all | solution.py:110
  40.0 3.7 %copy-start.5 = (s32[64]{0:T(128)S(1)}, s32[64]{0:T(128)}, u32[]{:S(2)}) copy-start(s32[64]{0:T(128)} %get-tuple-element.145) | copy-start | bytes 772 | tf_op jit(solution)/shard_map/while
  49.0 3.7 %copy-start.5 = (s32[64]{0:T(128)S(1)}, s32[64]{0:T(128)}, u32[]{:S(2)}) copy-start(s32[64]{0:T(128)} %get-tuple-element.145) | copy-start | bytes 772 | tf_op jit(solution)/shard_map/while
  58.1 3.7 %copy-start.5 = (s32[64]{0:T(128)S(1)}, s32[64]{0:T(128)}, u32[]{:S(2)}) copy-start(s32[64]{0:T(128)} %get-tuple-element.145) | copy-start | bytes 772 | tf_op jit(solution)/shard_map/while
  67.1 3.7 %copy-start.5 = (s32[64]{0:T(128)S(1)}, s32[64]{0:T(128)}, u32[]{:S(2)}) copy-start(s32[64]{0:T(128)} %get-tuple-element.145) | copy-start | bytes 772 | tf_op jit(solution)/shard_map/while
  75.5 20.1 %all-to-all-start.1 = ((bf16[4,64,1024]{2,0,1:T(4,128)(2,1)}), bf16[4,64,1024]{2,0,1:T(4,128)(2,1)S(1)}, u32[]{:S(2)}, u32[]{:S(2)}) async-start(bf16[4,64,1024]{2,0,1:T(4,128)(2,1)} %copy.37), calls=%async_computation.1 | async-start | bytes 1048576 | tf_op jit(solution)/shard_map/all_to_all | solution.py:126
  83.0 2.9 %copy-start.8 = (bf16[1024]{0:T(1024)(128)(2,1)S(1)}, bf16[1024]{0:T(1024)(128)(2,1)}, u32[]{:S(2)}) copy-start(bf16[1024]{0:T(1024)(128)(2,1)} %param.23) | copy-start | bytes 6148
  85.9 9.5 %copy-start.4 = (s32[8,128]{1,0:T(8,128)S(1)}, s32[8,128]{1,0:T(8,128)}, u32[]{:S(2)}) copy-start(s32[8,128]{1,0:T(8,128)} %param.29) | copy-start | bytes 12292
  85.9 9.5 %copy-start.6 = (pred[8,32]{1,0:T(8,128)(4,1)S(1)}, pred[8,32]{1,0:T(8,128)(4,1)}, u32[]{:S(2)}) copy-start(pred[8,32]{1,0:T(8,128)(4,1)} %broadcast_compare_fusion) | copy-start | bytes 772
  105.2 1.6 copy-start.9
  117.2 54.7 %copy-start.2 = (bf16[8,1024]{1,0:T(8,128)(2,1)}, bf16[8,1024]{1,0:T(8,128)(2,1)S(1)}, u32[]{:S(2)}) copy-start(bf16[8,1024]{1,0:T(8,128)(2,1)S(1)} %get-tuple-element.68) | copy-start | bytes 49156
  165.1 6.8 %copy-start.3 = (s32[8]{0:T(128)S(1)}, s32[8]{0:T(128)}, u32[]{:S(2)}) copy-start(s32[8]{0:T(128)} %or_bitcast_fusion) | copy-start | bytes 100
  165.1 7.6 %copy-start.11 = (s32[8]{0:T(128)S(1)}, s32[8]{0:T(128)}, u32[]{:S(2)}) copy-start(s32[8]{0:T(128)} %param.28) | copy-start | bytes 100
where the time goes:
time: 176 us; the launch traced here: 173 us
  blocking collectives  46.7 us (27%)
  local copies, waits for them, and re-layouts  46.4 us (26%)
  matrix products  25 us (14%)
  other arithmetic  22.1 us (13%)
  starting transfers between devices  15.8 us (9%)
  waiting for transfers between devices  15.6 us (9%)
    all_gather x1, blocking collectives, per_device(): lax.all_gather(embedding, 'parcel', axis=0, tiled=True).astype(jnp.float32)  46.7 us
    all_to_all x1, waiting for transfers between devices, per_device(): lax.all_to_all(tile_pixels, 'parcel', split_axis=1, concat_axis=1, tiled=...  15.6 us
    all_to_all x1, starting transfers between devices, per_device(): lax.all_to_all(tile_pixels, 'parcel', split_axis=1, concat_axis=1, tiled=...  11.3 us
    dot_general x4, matrix products, pool_pixels(): jnp.dot(hidden_one, w_pix2, preferred_element_type=jnp.float32)  11.3 us
    unnamed x25, local copies, waits for them, and re-layouts  11.3 us
    reshape x4, local copies, waits for them, and re-layouts, pool_pixels(): flattened = pixels.reshape(row_count * pix_width, channels)  9.3 us
    reduce_sum x4, other arithmetic, pool_pixels(): jnp.sum(valid_mask[:, :, None] * (hidden_two - center[:, None, :]) ** 2,...  7.72 us
    gather x1, local copies, waits for them, and re-layouts, contrast(): negative = jnp.take_along_axis(similarity, neg_ids, axis=1) * logit_scale[0]  6.78 us
  transfers between devices with their start and end apart: 2, of which 1 were waited for; matrix products, arithmetic and copies ran while one was open for 11% of the time, Pallas kernels for 0%

commit v1 on v0

v1 whole, which is shorter than its diff:
```python
import jax
import jax.numpy as jnp
import numpy as np
from jax import lax
from jax.experimental import pallas as pl
from jax.experimental.pallas import tpu as pltpu
from jax.sharding import PartitionSpec as P

PAR_DEV = 64
CAP = 4
SETS = 64
BF = jnp.bfloat16
F32 = jnp.float32
I32 = jnp.int32
LOG2E = 1.4426950408889634


def iota(shape, dim):
    return lax.broadcasted_iota(I32, shape, dim)


def mm(left, right):
    return jnp.dot(left, right, preferred_element_type=F32)


def mm_nt(left, right):
    return lax.dot_general(left, right, (((1,), (1,)), ((), ())), preferred_element_type=F32)


def rep(block, times):
    return jnp.concatenate([block] * times, axis=0)


def pool_kernel(tile_ref, x_ref, own_ref, cnt_ref, w1_ref, w2_ref, out_ref, w1s, ps):
    rows = 4 * 128
    match = own_ref[...] == tile_ref[0]
    li = iota((128, 128), 0)
    lj = iota((128, 128), 1)
    before = ((li < lj) & ((li // 64) == (lj // 64))).astype(BF)
    rank = mm(match.astype(F32).astype(BF), before)
    code = jnp.where(match, rank.astype(I32), -1)
    sub = iota((16, 8, 128), 1)
    lane = iota((16, 8, 128), 2)
    hit = (code[:, None, :] == (sub % 4)) & ((lane // 64) == (sub // 4))
    amount = jnp.where(hit, cnt_ref[...][:, None, :], 0).reshape(128, 128)
    counts = mm(amount.astype(F32).astype(BF), jnp.ones((128, 128), BF))

    channel = (iota((640, 16), 0) % 10 == iota((640, 16), 1)).astype(BF)
    w1 = jnp.concatenate([w1_ref[...].astype(F32), jnp.zeros((6, 128), F32)], axis=0)
    tiled = mm(channel, w1.astype(BF))
    windows = []
    for j in range(SETS // 2):
        low = 20 * j
        start = low // 128 * 128
        depth = 256 if low + 20 > start + 128 else 128
        windows.append((start, depth))
        part = tiled[start : start + depth]
        row = iota((depth, 128), 0) + start
        w1s[j, 0:depth, 0:128] = jnp.where((row >= low) & (row < low + 10), part, 0.0).astype(BF)
        w1s[j, 0:depth, 128:256] = jnp.where(
            (row >= low + 10) & (row < low + 20), part, 0.0
        ).astype(BF)
    zero = jnp.zeros((128, 128), BF)
    w2 = w2_ref[...]
    w2 = jnp.concatenate(
        [jnp.concatenate([w2, zero], axis=1), jnp.concatenate([zero, w2], axis=1)], axis=0
    )

    x = x_ref[...].reshape(rows, 640)
    valid = (iota((128, 640), 1) // 10).astype(F32) < jnp.concatenate([counts] * 5, axis=1)
    to_all = ((iota((128, 640), 1) % 10) == iota((128, 640), 0)).astype(BF)
    first = mm(x[:, 0:128], to_all)
    ps[...] = jnp.where(rep(valid, 4), x.astype(F32), first).astype(BF)
    origin = total = square = None
    for j, (start, depth) in enumerate(windows):
        hidden = mm(ps[:, start : start + depth], w1s[j, 0:depth, :])
        hidden = jnp.maximum(hidden.astype(BF), 0)
        hidden = jnp.maximum(mm(hidden, w2), 0.0)
        if j == 0:
            origin = hidden[:, 0:128]
            total = hidden[:, 128:256] - origin
            square = total * total
        else:
            even = hidden[:, 0:128] - origin
            odd = hidden[:, 128:256] - origin
            total = total + (even + odd)
            square = square + (even * even + odd * odd)
    number = jnp.maximum(rep(counts, 4), 1.0)
    shift = total / number
    deviation = jnp.sqrt(jnp.maximum(square / number - shift * shift, 0.01))
    pooled = jnp.concatenate([origin + shift, deviation], axis=1).astype(BF)
    po = iota((256, 256), 0)
    pi = iota((256, 256), 1)
    order = ((po // 16 == pi // 4 % 16) & (po // 4 % 4 == pi // 64) & (po % 4 == pi % 4)).astype(BF)
    for half in range(2):
        part = jnp.concatenate(
            [pooled[d * 128 + half * 64 : d * 128 + half * 64 + 64] for d in range(4)], axis=0
        )
        out_ref[half * 16 : half * 16 + 16] = mm(order, part).astype(BF).reshape(16, 16, 256)


def pool_slots(tile, pixels, owner, counts, w_pix1, w_pix2):
    vmem = pl.BlockSpec(memory_space=pltpu.VMEM)
    return pl.pallas_call(
        pool_kernel,
        out_shape=jax.ShapeDtypeStruct((32, 16, 256), BF),
        in_specs=[pl.BlockSpec(memory_space=pltpu.SMEM)] + [vmem] * 5,
        out_specs=vmem,
        scratch_shapes=[pltpu.VMEM((32, 256, 256), BF), pltpu.VMEM((512, 640), BF)],
        compiler_params=pltpu.CompilerParams(vmem_limit_bytes=40 << 20),
        name="pool_slots",
    )(tile, pixels, owner, counts, w_pix1, w_pix2)


def attend_kernel(
    tok_ref, clear_ref, code_ref, gain_ref, scale_ref, we_ref, wqkv_ref, wo_ref, emb_ref, all_ref
):
    encoded = mm(tok_ref[...], we_ref[...]).astype(BF).astype(F32)
    code = jnp.broadcast_to(code_ref[...][:, None, :], (32, 8, 1024)).reshape(256, 1024)
    state = encoded + code
    state_mean = jnp.mean(state.reshape(32, 8, 1024), axis=0)
    center = jnp.mean(state, axis=1, keepdims=True)
    moved = state - center
    spread = jnp.mean(moved * moved, axis=1, keepdims=True)
    normed = (moved * lax.rsqrt(spread + 1e-05) * gain_ref[...].astype(F32)).astype(BF)

    seg = (iota((256, 256), 0) // 64 == iota((256, 256), 1) // 64).astype(BF)
    qi = iota((256, 256), 0)
    ki = iota((256, 256), 1)
    mask = jnp.where(
        (qi % 8 == ki % 8) & ((qi == ki) | (clear_ref[...] > 0.0)), jnp.float32(1), jnp.float32(0)
    )
    left = iota((256, 128), 1) < 64
    ones = jnp.ones((256, 128), BF)
    none = jnp.zeros((256, 128), BF)
    means = []
    for c in range(4):
        span = slice(256 * c, 256 * c + 256)
        queries = mm(normed, wqkv_ref[:, 256 * c : 256 * c + 256])
        keys = mm(normed, wqkv_ref[:, 1024 + 256 * c : 1024 + 256 * c + 256])
        values = mm(normed, wqkv_ref[:, 2048 + 256 * c : 2048 + 256 * c + 256]).astype(BF)
        q_sum = mm((queries * queries).astype(BF), seg)
        k_sum = mm((keys * keys).astype(BF), seg)
        queries = (queries * (lax.rsqrt(q_sum + 1e-06) * (scale_ref[:, span] * LOG2E))).astype(BF)
        keys = (keys * lax.rsqrt(k_sum + 1e-06)).astype(BF)
        for pair in range(2):
            lanes = slice(128 * pair, 128 * pair + 128)
            q_pair = queries[:, lanes]
            k_pair = keys[:, lanes]
            right = jnp.concatenate([values[:, lanes], ones], axis=1)
            mixed = []
            for side in range(2):
                k_side = jnp.where(left, k_pair, none) if side == 0 else jnp.where(left, none, k_pair)
                weights = (jnp.exp2(mm_nt(q_pair, k_side)) * mask).astype(BF)
                both = mm(weights, right)
                mixed.append(both[:, 0:128] / both[:, 128:256])
            means.append(jnp.mean(jnp.where(left, mixed[0], mixed[1]).reshape(32, 8, 128), axis=0))
    mean = jnp.concatenate(means, axis=1)
    high = mean.astype(BF)
    low = (mean - high.astype(F32)).astype(BF)
    update = mm(jnp.concatenate([high, low], axis=0), wo_ref[...])
    embedding = (state_mean + (update[0:8] + update[8:16])).astype(BF)
    emb_ref[...] = embedding
    all_ref[...] = jnp.broadcast_to(embedding[None], (32, 8, 1024))


def attend(tokens, clear, code, gain, scale, w_embed, w_qkv, w_out):
    vmem = pl.BlockSpec(memory_space=pltpu.VMEM)
    return pl.pallas_call(
        attend_kernel,
        out_shape=(
            jax.ShapeDtypeStruct((8, 1024), BF),
            jax.ShapeDtypeStruct((32, 8, 1024), BF),
        ),
        in_specs=[vmem] * 8,
        out_specs=(vmem, vmem),
        compiler_params=pltpu.CompilerParams(vmem_limit_bytes=40 << 20),
        name="attend",
    )(tokens, clear, code, gain, scale, w_embed, w_qkv, w_out)


def contrast_kernel(scale_ref, emb_ref, all_ref, pos_ref, neg_ref, out_ref):
    others = all_ref[...].astype(F32)
    square = others * others
    high = square.astype(BF)
    low = (square - high.astype(F32)).astype(BF)
    ones = jnp.ones((8, 1024), BF)
    other_sum = mm_nt(ones, high) + mm_nt(ones, low)
    anchors = emb_ref[...].astype(F32)
    own_sum = jnp.sum(anchors * anchors, axis=1, keepdims=True)
    similarity = mm_nt(emb_ref[...], all_ref[...])
    similarity = similarity * lax.rsqrt(own_sum + 1e-06) * lax.rsqrt(other_sum + 1e-06)
    logits = similarity * scale_ref[0]
    member = iota((8, 256), 1)
    positive = jnp.sum(jnp.where(member == pos_ref[...], logits, 0.0), axis=1, keepdims=True)
    ids = neg_ref[...]
    within = ids % 128
    near = jnp.take_along_axis(logits[:, 0:128], within, axis=1)
    far = jnp.take_along_axis(logits[:, 128:256], within, axis=1)
    negative = jnp.where(ids < 128, near, far)
    loss = jnp.log(1.0 + jnp.sum(jnp.exp(negative - positive), axis=1, keepdims=True))
    diagonal = iota((8, 128), 0) == iota((8, 128), 1)
    out_ref[...] = jnp.sum(jnp.where(diagonal, loss, 0.0), axis=0, keepdims=True)[:, 0:8]


def contrast(scale, embedding, others, pos_ids, neg_ids):
    vmem = pl.BlockSpec(memory_space=pltpu.VMEM)
    return pl.pallas_call(
        contrast_kernel,
        out_shape=jax.ShapeDtypeStruct((1, 8), F32),
        in_specs=[pl.BlockSpec(memory_space=pltpu.SMEM)] + [vmem] * 4,
        out_specs=vmem,
        compiler_params=pltpu.CompilerParams(vmem_limit_bytes=16 << 20),
        name="contrast",
    )(scale, embedding, others, pos_ids, neg_ids)


def date_code(dates, width):
    steps = np.arange(dates, dtype=np.float64)[:, None]
    pair = np.arange(width // 2, dtype=np.float64)[None, :]
    angles = steps * np.exp(-2.0 * pair / width * np.log(10000.0))
    table = np.stack([np.sin(angles), np.cos(angles)], axis=-1).reshape(dates, width)
    return table.astype(np.float32)


def slot_matrix(block_owner):
    place = jnp.arange(PAR_DEV, dtype=I32)
    same = (block_owner[:, None] == block_owner[None, :]) & (place[None, :] < place[:, None])
    rank = jnp.sum(same.astype(I32), axis=1)
    source = (block_owner * 16 + rank).reshape(8, 1, 8) + 4 * jnp.arange(4, dtype=I32)[None, :, None]
    return (source.reshape(256, 1) == jnp.arange(512, dtype=I32)[None, :]).astype(BF)


def per_device(
    tile_pixels,
    owner,
    pix_count,
    cloud,
    w_pix1,
    w_pix2,
    w_embed,
    norm_gain,
    w_qkv,
    w_out,
    head_scale,
    logit_scale,
    pos_ids,
    neg_ids,
):
    block = lax.axis_index("parcel")
    pooled = pool_slots(
        block.reshape(1).astype(I32),
        tile_pixels,
        owner.reshape(16, 128),
        pix_count.reshape(16, 128),
        w_pix1,
        w_pix2,
    )
    arrived = lax.all_to_all(pooled, "parcel", split_axis=0, concat_axis=0, tiled=True)
    pick = slot_matrix(lax.dynamic_slice_in_dim(owner[:, 0], block * PAR_DEV, PAR_DEV))
    moving = mm(pick, arrived.reshape(512, 256)).astype(BF).reshape(8, 32, 256)
    tokens = lax.all_to_all(moving, "date", split_axis=0, concat_axis=0, tiled=True)
    embedding, copies = attend(
        tokens.reshape(256, 256),
        (cloud.T == 0).astype(F32).reshape(1, 256),
        jnp.asarray(date_code(32, 1024)),
        norm_gain.reshape(1, 1024),
        jnp.repeat(head_scale, 64).reshape(1, 1024),
        w_embed,
        w_qkv,
        w_out,
    )
    others = lax.all_to_all(copies, "parcel", split_axis=0, concat_axis=0, tiled=True)
    loss = contrast(
        logit_scale, embedding, others.reshape(256, 1024), pos_ids.reshape(8, 1), neg_ids
    )
    return (embedding, loss.reshape(8))


def solution(mesh):
    in_specs = (
        P("date", "parcel", None),
        P(),
        P(),
        P(("parcel", "date"), None),
        P(),
        P(),
        P(),
        P(),
        P(),
        P(),
        P(),
        P(),
        P(("parcel", "date")),
        P(("parcel", "date"), None),
    )
    out_specs = (P(("parcel", "date"), None), P(("parcel", "date")))
    return jax.shard_map(
        per_device, mesh=mesh, in_specs=in_specs, out_specs=out_specs, check_vma=False
    )
```

time: 176 us -> 82.7 us (0.47)
  blocking collectives: 46.7 us -> 0 us
  local copies, waits for them, and re-layouts: 46.4 us -> 13 us
  matrix products: 25 us -> 0.93 us
  other arithmetic: 22.1 us -> 1.7 us
  waiting for transfers between devices: 15.6 us -> 31.5 us
  Pallas kernels: 0 us -> 13.2 us
  starting transfers between devices: 15.8 us -> 20.2 us
    all_gather x1 -> x0, blocking collectives: 46.7 us -> none  [per_device(): lax.all_gather(embedding, 'parcel', axis=0, tiled=True).astype(jnp.float32)]
    dot_general x10 -> x1, matrix products: 25 us -> 0.93 us  [mm(): return jnp.dot(left, right, preferred_element_type=F32)]
    all_to_all x2 -> x3, waiting for transfers between devices: 15.6 us -> 31.5 us  [the longest x1 16.7 us: per_device(): lax.all_to_all(copies, 'parcel', split_axis=0, concat_axis=0, tiled=True)]
    pallas_call x0 -> x3, Pallas kernels: none -> 13.2 us  [the longest x1 6.29 us: pool_slots(): pl.pallas_call(pool_kernel, out_shape=jax.ShapeDtypeStruct((32, 16, 256),...]
    reduce_sum x12 -> x1, other arithmetic: 12 us -> 0.17 us  [slot_matrix(): rank = jnp.sum(same.astype(I32), axis=1)]
    reshape x5 -> x4, local copies, waits for them, and re-layouts: 10.5 us -> 0.94 us  [the longest x1 0.69 us: per_device(): norm_gain.reshape(1, 1024)]
    gather x3 -> x0, local copies, waits for them, and re-layouts: 8.29 us -> none  [the longest x1 6.78 us: contrast(): negative = jnp.take_along_axis(similarity, neg_ids, axis=1) * logit_scale[0]]
    add x3 -> x1, local copies, waits for them, and re-layouts: 5.81 us -> 0.1 us  [slot_matrix(): (block_owner * 16 + rank).reshape(8, 1, 8)]
  transfers between devices with their start and end apart: 2 -> 3, of which waited for: 1 -> 3; matrix products, arithmetic and copies ran while one was open for 11% -> 5% of each run, Pallas kernels for 0% -> 0%
where the time goes in v1:
time: 82.7 us; the launch traced here: 81.9 us
  waiting for transfers between devices  31.5 us (38%)
  starting transfers between devices  20.2 us (24%)
  Pallas kernels  13.2 us (16%)
  local copies, waits for them, and re-layouts  13 us (16%)
  other arithmetic  1.7 us (2%)
  between operations  1.36 us (2%)
  matrix products  0.93 us (1%)
    all_to_all x1, waiting for transfers between devices, per_device(): lax.all_to_all(copies, 'parcel', split_axis=0, concat_axis=0, tiled=True)  16.7 us
    all_to_all x1, starting transfers between devices, per_device(): lax.all_to_all(pooled, 'parcel', split_axis=0, concat_axis=0, tiled=True)  11.2 us
    all_to_all x1, waiting for transfers between devices, per_device(): lax.all_to_all(pooled, 'parcel', split_axis=0, concat_axis=0, tiled=True)  11 us
    unnamed x24, local copies, waits for them, and re-layouts  11 us
    pallas_call x1, Pallas kernels, pool_slots(): pl.pallas_call(pool_kernel, out_shape=jax.ShapeDtypeStruct((32, 16, 256),...  6.29 us
    pallas_call x1, Pallas kernels, attend(): pl.pallas_call(attend_kernel, out_shape=(jax.ShapeDtypeStruct((8, 1024),...  5.68 us
    all_to_all x1, starting transfers between devices, per_device(): lax.all_to_all(copies, 'parcel', split_axis=0, concat_axis=0, tiled=True)  4.55 us
    all_to_all x1, starting transfers between devices, per_device(): lax.all_to_all(moving, 'date', split_axis=0, concat_axis=0, tiled=True)  4.47 us
  transfers between devices with their start and end apart: 3, of which 3 were waited for; matrix products, arithmetic and copies ran while one was open for 5% of the time, Pallas kernels for 0%

profile of v1, /device:TPU:32, one launch (start us, length us, event | category | flops | bytes accessed | tf_op | source)
XLA Modules:
  0.0 81.9 jit_solution(13250297504220240447)
XLA Ops:
  0.6 0.0 copy-start.2
  0.6 1.1 %copy-done.2 = bf16[4,128,640]{2,1,0:T(8,128)(2,1)S(1)} copy-done((bf16[4,128,640]{2,1,0:T(8,128)(2,1)S(1)}, bf16[4,128,640]{2,1,0:T(8,128)(2,1)}, u32[]{:S(2)}) %copy-start.2) | copy-done | bytes 655384
  1.7 0.0 copy-start.5
  1.7 0.8 copy-done.5
  2.5 0.0 copy-start.7
  2.5 0.7 copy-done.7
  3.2 0.0 copy-start.8
  3.2 0.7 copy-done.8
  3.9 0.0 copy-start.9
  3.9 0.7 copy-done.9
  4.6 0.0 copy-start.11
  4.6 0.0 copy-start.10
  4.6 6.3 %pool_slots.1 = bf16[32,16,256]{2,1,0:T(8,128)(2,1)} custom-call(s32[1]{0:T(128)} %bitcast.1.tile_ref, bf16[4,128,640]{2,1,0:T(8,128)(2,1)S(1)} %copy-done.2, s32[16,128]{1,0:T(8,128)S(1)} %bitcast.16, s32[16,128]{1,0:T(8,128)S(1)} %bitcast.17, bf16[10,128]{1,0:T(8,128)(2,1)S(1)} %copy-done.9, bf16[128,128]{1,0:T(8,128)(2,1)S(1)} %copy-done.5), custom_call_target="tpu_custom_call" | custom-call | tf_op jit(solution)/shard_map/pool_slots/pallas_call | solution.py:104
  10.9 11.2 %all-to-all-start = ((bf16[32,16,256]{2,1,0:T(8,128)(2,1)}), bf16[32,16,256]{2,1,0:T(8,128)(2,1)S(1)}, u32[]{:S(2)}, u32[]{:S(2)}) async-start(bf16[32,16,256]{2,1,0:T(8,128)(2,1)} %pool_slots.1), calls=%async_computation | async-start | bytes 524288 | tf_op jit(solution)/shard_map/all_to_all | solution.py:259
  22.1 0.7 fusion.2
  22.8 0.2 convert_reduce_fusion
  23.0 0.1 reduce_sum.12
  23.1 0.1 mul.27
  23.2 0.1 broadcast_add_fusion
  23.2 0.1 add.35
  23.3 11.0 %all-to-all-done = bf16[32,16,256]{2,1,0:T(8,128)(2,1)S(1)} async-done(((bf16[32,16,256]{2,1,0:T(8,128)(2,1)}), bf16[32,16,256]{2,1,0:T(8,128)(2,1)S(1)}, u32[]{:S(2)}, u32[]{:S(2)}) %all-to-all-start) | async-done | bytes 262176 | tf_op jit(solution)/shard_map/all_to_all | solution.py:259
  34.3 0.9 %convolution_convert_fusion = bf16[256,256]{1,0:T(8,128)(2,1)} fusion(bf16[512,256]{1,0:T(8,128)(2,1)S(1)} %bitcast.18, s32[256]{0:T(256)S(1)} %add.35), kind=kOutput, calls=%fused_computation | convolution fusion | flops 67305472 | bytes 394240 | tf_op jit(solution)/shard_map/dot_general | solution.py:23
  35.3 4.5 %all-to-all-start.1 = ((bf16[8,32,256]{2,1,0:T(8,128)(2,1)}), bf16[8,32,256]{2,1,0:T(8,128)(2,1)S(1)}, u32[]{:S(2)}, u32[]{:S(2)}) async-start(bf16[8,32,256]{2,1,0:T(8,128)(2,1)} %bitcast.5), calls=%async_computation.1 | async-start | bytes 262144 | tf_op jit(solution)/shard_map/all_to_all | solution.py:262
  39.7 0.7 convert_bitcast_fusion
  40.4 0.1 copy.21
  40.5 0.1 reshape.89.clear_ref
  40.6 0.7 broadcast_in_dim.2
  41.3 0.1 reshape_reshape.3.scale_ref
  41.4 0.7 reshape.84.gain_ref
  42.1 3.8 %all-to-all-done.1 = bf16[8,32,256]{2,1,0:T(8,128)(2,1)S(1)} async-done(((bf16[8,32,256]{2,1,0:T(8,128)(2,1)}), bf16[8,32,256]{2,1,0:T(8,128)(2,1)S(1)}, u32[]{:S(2)}, u32[]{:S(2)}) %all-to-all-start.1) | async-done | bytes 131104 | tf_op jit(solution)/shard_map/all_to_all | solution.py:262
  45.9 0.0 copy-start
  45.9 2.8 %copy-done = bf16[1024,3072]{1,0:T(8,128)(2,1)S(1)} copy-done((bf16[1024,3072]{1,0:T(8,128)(2,1)S(1)}, bf16[1024,3072]{1,0:T(8,128)(2,1)}, u32[]{:S(2)}) %copy-start) | copy-done | bytes 6291480
  48.7 0.0 copy-start.1
  48.7 1.6 %copy-done.1 = bf16[1024,1024]{1,0:T(8,128)(2,1)S(1)} copy-done((bf16[1024,1024]{1,0:T(8,128)(2,1)S(1)}, bf16[1024,1024]{1,0:T(8,128)(2,1)}, u32[]{:S(2)}) %copy-start.1) | copy-done | bytes 2097176
  50.3 0.0 copy-start.3
  50.3 1.0 %copy-done.3 = bf16[256,1024]{1,0:T(8,128)(2,1)S(1)} copy-done((bf16[256,1024]{1,0:T(8,128)(2,1)S(1)}, bf16[256,1024]{1,0:T(8,128)(2,1)}, u32[]{:S(2)}) %copy-start.3) | copy-done | bytes 524312
  51.3 0.0 copy-start.4
  51.3 0.9 %copy-done.4 = f32[32,1024]{1,0:T(8,128)S(1)} copy-done((f32[32,1024]{1,0:T(8,128)S(1)}, f32[32,1024]{1,0:T(8,128)}, u32[]{:S(2)}) %copy-start.4) | copy-done | bytes 131096
  52.2 5.7 %attend.1 = (bf16[8,1024]{1,0:T(8,128)(2,1)}, bf16[32,8,1024]{2,1,0:T(8,128)(2,1)}) custom-call(bf16[256,256]{1,0:T(8,128)(2,1)S(1)} %bitcast.15, f32[1,256]{1,0:T(1,128)S(1)} %reshape.89.clear_ref, f32[32,1024]{1,0:T(8,128)S(1)} %copy-done.4, bf16[1,1024]{1,0:T(2,128)(2,1)S(1)} %reshape.84.gain_ref, f32[1,1024]{1,0:T(1,128)S(1)} %reshape_reshape.3.scale_ref, ...), custom_call_target="tpu_custom_call" | custom-call | tf_op jit(solution)/shard_map/attend/pallas_call | solution.py:169
  57.9 4.6 %all-to-all-start.2 = ((bf16[32,8,1024]{2,1,0:T(8,128)(2,1)}), bf16[32,8,1024]{2,1,0:T(8,128)(2,1)S(1)}, u32[]{:S(2)}, u32[]{:S(2)}) async-start(bf16[32,8,1024]{2,1,0:T(8,128)(2,1)} %get-tuple-element.5), calls=%async_computation.2 | async-start | bytes 1048576 | tf_op jit(solution)/shard_map/all_to_all | solution.py:273
  62.4 0.0 copy-done.11
  62.5 0.1 copy.22.pos_ref
  63.2 16.7 %all-to-all-done.2 = bf16[32,8,1024]{2,1,0:T(8,128)(2,1)S(1)} async-done(((bf16[32,8,1024]{2,1,0:T(8,128)(2,1)}), bf16[32,8,1024]{2,1,0:T(8,128)(2,1)S(1)}, u32[]{:S(2)}, u32[]{:S(2)}) %all-to-all-start.2) | async-done | bytes 524320 | tf_op jit(solution)/shard_map/all_to_all | solution.py:273
  79.9 0.0 copy-done.10
  79.9 0.0 copy-start.6
  79.9 0.7 copy-done.6
  80.6 1.3 %contrast.1 = f32[1,8]{1,0:T(1,128)} custom-call(f32[1]{0:T(128)S(6)} %copy.23.scale_ref, bf16[8,1024]{1,0:T(8,128)(2,1)S(1)} %copy-done.6, bf16[256,1024]{1,0:T(8,128)(2,1)S(1)} %bitcast.14, s32[8,1]{1,0:T(8,128)S(1)} %copy.22.pos_ref, s32[8,128]{1,0:T(8,128)S(1)} %copy-done.10), custom_call_target="tpu_custom_call" | custom-call | tf_op jit(solution)/shard_map/contrast/pallas_call | solution.py:208
  (2 shorter events, 0.0 us)
Async XLA Ops:
  0.6 1.1 %copy-start.2 = (bf16[4,128,640]{2,1,0:T(8,128)(2,1)S(1)}, bf16[4,128,640]{2,1,0:T(8,128)(2,1)}, u32[]{:S(2)}) copy-start(bf16[4,128,640]{2,1,0:T(8,128)(2,1)} %x_ref.1) | copy-start | bytes 1966084
  1.7 0.8 copy-start.5
  2.5 0.7 copy-start.7
  3.2 0.7 copy-start.8
  3.9 0.7 copy-start.9
  4.6 57.9 %copy-start.11 = (s32[8]{0:T(128)S(1)}, s32[8]{0:T(128)}, u32[]{:S(2)}) copy-start(s32[8]{0:T(128)} %param.27) | copy-start | bytes 100
  4.6 75.3 %copy-start.10 = (s32[8,128]{1,0:T(8,128)S(1)}, s32[8,128]{1,0:T(8,128)}, u32[]{:S(2)}) copy-start(s32[8,128]{1,0:T(8,128)} %neg_ref.1) | copy-start | bytes 12292
  10.9 23.5 %all-to-all-start = ((bf16[32,16,256]{2,1,0:T(8,128)(2,1)}), bf16[32,16,256]{2,1,0:T(8,128)(2,1)S(1)}, u32[]{:S(2)}, u32[]{:S(2)}) async-start(bf16[32,16,256]{2,1,0:T(8,128)(2,1)} %pool_slots.1), calls=%async_computation | async-start | bytes 524288 | tf_op jit(solution)/shard_map/all_to_all | solution.py:259
  35.3 10.6 %all-to-all-start.1 = ((bf16[8,32,256]{2,1,0:T(8,128)(2,1)}), bf16[8,32,256]{2,1,0:T(8,128)(2,1)S(1)}, u32[]{:S(2)}, u32[]{:S(2)}) async-start(bf16[8,32,256]{2,1,0:T(8,128)(2,1)} %bitcast.5), calls=%async_computation.1 | async-start | bytes 262144 | tf_op jit(solution)/shard_map/all_to_all | solution.py:262
  45.9 2.8 %copy-start = (bf16[1024,3072]{1,0:T(8,128)(2,1)S(1)}, bf16[1024,3072]{1,0:T(8,128)(2,1)}, u32[]{:S(2)}) copy-start(bf16[1024,3072]{1,0:T(8,128)(2,1)} %wqkv_ref.1) | copy-start | bytes 18874372
  48.7 1.6 %copy-start.1 = (bf16[1024,1024]{1,0:T(8,128)(2,1)S(1)}, bf16[1024,1024]{1,0:T(8,128)(2,1)}, u32[]{:S(2)}) copy-start(bf16[1024,1024]{1,0:T(8,128)(2,1)} %wo_ref.1) | copy-start | bytes 6291460
  50.3 1.0 %copy-start.3 = (bf16[256,1024]{1,0:T(8,128)(2,1)S(1)}, bf16[256,1024]{1,0:T(8,128)(2,1)}, u32[]{:S(2)}) copy-start(bf16[256,1024]{1,0:T(8,128)(2,1)} %we_ref.1) | copy-start | bytes 1572868
  51.3 0.9 %copy-start.4 = (f32[32,1024]{1,0:T(8,128)S(1)}, f32[32,1024]{1,0:T(8,128)}, u32[]{:S(2)}) copy-start(f32[32,1024]{1,0:T(8,128)} %constant.18.clone.code_ref) | copy-start | bytes 393220
  57.9 22.0 %all-to-all-start.2 = ((bf16[32,8,1024]{2,1,0:T(8,128)(2,1)}), bf16[32,8,1024]{2,1,0:T(8,128)(2,1)S(1)}, u32[]{:S(2)}, u32[]{:S(2)}) async-start(bf16[32,8,1024]{2,1,0:T(8,128)(2,1)} %get-tuple-element.5), calls=%async_computation.2 | async-start | bytes 1048576 | tf_op jit(solution)/shard_map/all_to_all | solution.py:273
  79.9 0.7 copy-start.6

commit v2 on v1

--- a/solution.py
+++ b/solution.py
@@ -31,7 +31,16 @@
     return jnp.concatenate([block] * times, axis=0)
 
 
-def pool_kernel(tile_ref, x_ref, own_ref, cnt_ref, w1_ref, w2_ref, out_ref, w1s, ps):
+def pool_kernel(
+    tile_ref, x_any, own_any, cnt_any, w1_any, w2_any, out_ref,
+    x_ref, own_ref, cnt_ref, w1_ref, w2_ref, w1s, ps, sems,
+):
+    pairs = [(own_any, own_ref), (cnt_any, cnt_ref), (w1_any, w1_ref), (w2_any, w2_ref), (x_any, x_ref)]
+    copies = [pltpu.make_async_copy(a, b, sems.at[i]) for i, (a, b) in enumerate(pairs)]
+    for copy in copies:
+        copy.start()
+    copies[0].wait()
+    copies[1].wait()
     rows = 4 * 128
     match = own_ref[...] == tile_ref[0]
     li = iota((128, 128), 0)
@@ -45,6 +54,7 @@
     amount = jnp.where(hit, cnt_ref[...][:, None, :], 0).reshape(128, 128)
     counts = mm(amount.astype(F32).astype(BF), jnp.ones((128, 128), BF))
 
+    copies[2].wait()
     channel = (iota((640, 16), 0) % 10 == iota((640, 16), 1)).astype(BF)
     w1 = jnp.concatenate([w1_ref[...].astype(F32), jnp.zeros((6, 128), F32)], axis=0)
     tiled = mm(channel, w1.astype(BF))
@@ -61,11 +71,13 @@
             (row >= low + 10) & (row < low + 20), part, 0.0
         ).astype(BF)
     zero = jnp.zeros((128, 128), BF)
+    copies[3].wait()
     w2 = w2_ref[...]
     w2 = jnp.concatenate(
         [jnp.concatenate([w2, zero], axis=1), jnp.concatenate([zero, w2], axis=1)], axis=0
     )
 
+    copies[4].wait()
     x = x_ref[...].reshape(rows, 640)
     valid = (iota((128, 640), 1) // 10).astype(F32) < jnp.concatenate([counts] * 5, axis=1)
     to_all = ((iota((128, 640), 1) % 10) == iota((128, 640), 0)).astype(BF)
@@ -100,21 +112,103 @@
 
 
 def pool_slots(tile, pixels, owner, counts, w_pix1, w_pix2):
-    vmem = pl.BlockSpec(memory_space=pltpu.VMEM)
     return pl.pallas_call(
         pool_kernel,
         out_shape=jax.ShapeDtypeStruct((32, 16, 256), BF),
-        in_specs=[pl.BlockSpec(memory_space=pltpu.SMEM)] + [vmem] * 5,
-        out_specs=vmem,
-        scratch_shapes=[pltpu.VMEM((32, 256, 256), BF), pltpu.VMEM((512, 640), BF)],
-        compiler_params=pltpu.CompilerParams(vmem_limit_bytes=40 << 20),
+        in_specs=[pl.BlockSpec(memory_space=pltpu.SMEM)] + [pl.BlockSpec(memory_space=pl.ANY)] * 5,
+        out_specs=pl.BlockSpec(memory_space=pltpu.VMEM),
+        scratch_shapes=[
+            pltpu.VMEM((4, 128, 640), BF),
+            pltpu.VMEM((16, 128), I32),
+            pltpu.VMEM((16, 128), I32),
+            pltpu.VMEM((10, 128), BF),
+            pltpu.VMEM((128, 128), BF),
+            pltpu.VMEM((32, 256, 256), BF),
+            pltpu.VMEM((512, 640), BF),
+            pltpu.SemaphoreType.DMA((5,)),
+        ],
+        compiler_params=pltpu.CompilerParams(vmem_limit_bytes=60 << 20),
         name="pool_slots",
     )(tile, pixels, owner, counts, w_pix1, w_pix2)
 
 
+def prepare_kernel(
+    block_ref, after, own_any, cloud_any, code_any, we_any,
+    pick_ref, mask_ref, code_ref, we_ref, own_ref, cloud_ref, sems,
+):
+    pairs = [
+        (own_any, own_ref),
+        (cloud_any, cloud_ref),
+        (we_any, we_ref),
+        (code_any, code_ref),
+    ]
+    copies = [pltpu.make_async_copy(a, b, sems.at[i]) for i, (a, b) in enumerate(pairs)]
+    for copy in copies:
+        copy.start()
+    copies[0].wait()
+    copies[1].wait()
+    block = block_ref[0]
+    owner = own_ref[pl.ds(block // 2, 1), :].astype(F32)
+    sub = iota((128, 128), 0)
+    lane = iota((128, 128), 1)
+    column = jnp.sum(jnp.where(sub == lane, owner, 0.0), axis=1, keepdims=True)
+    earlier = (column == owner) & (sub < lane) & (sub // 64 == lane // 64)
+    rank = jnp.sum(jnp.where(earlier, 1.0, 0.0), axis=0, keepdims=True)
+    source = owner * 16.0 + rank
+    row = iota((256, 128), 0)
+    parcel = (block % 2) * 64 + row // 32 * 8 + row % 8
+    wanted = jnp.sum(jnp.where(iota((256, 128), 1) == parcel, source, 0.0), axis=1, keepdims=True)
+    wanted = wanted.astype(I32) + iota((256, 1), 0) // 8 % 4 * 4
+    pick_ref[...] = jnp.where(iota((256, 512), 1) == wanted, 1.0, 0.0).astype(BF)
+    dates = (iota((32, 256), 1) // 8 == iota((32, 256), 0)).astype(BF)
+    clouds = mm(cloud_ref[...].astype(F32).astype(BF), dates)
+    own_row = iota((8, 256), 0) == iota((8, 256), 1) % 8
+    cloudy = jnp.sum(jnp.where(own_row, clouds, 0.0), axis=0, keepdims=True)
+    qi = iota((256, 256), 0)
+    ki = iota((256, 256), 1)
+    mask_ref[...] = jnp.where((qi % 8 == ki % 8) & ((qi == ki) | (cloudy == 0.0)), 1.0, 0.0)
+    for copy in copies[2:]:
+        copy.wait()
+
+
+def prepare(block, after, owner, cloud, code, w_embed):
+    kept = (code, w_embed)
+    return pl.pallas_call(
+        prepare_kernel,
+        out_shape=(
+            jax.ShapeDtypeStruct((256, 512), BF),
+            jax.ShapeDtypeStruct((256, 256), F32),
+        )
+        + tuple(jax.ShapeDtypeStruct(a.shape, a.dtype) for a in kept),
+        in_specs=[pl.BlockSpec(memory_space=pltpu.SMEM)] + [pl.BlockSpec(memory_space=pl.ANY)] * 5,
+        out_specs=(pl.BlockSpec(memory_space=pltpu.VMEM),) * 4,
+        scratch_shapes=[
+            pltpu.VMEM((16, 128), I32),
+            pltpu.VMEM((8, 32), I32),
+            pltpu.SemaphoreType.DMA((4,)),
+        ],
+        compiler_params=pltpu.CompilerParams(vmem_limit_bytes=48 << 20),
+        cost_estimate=pl.CostEstimate(flops=0, bytes_accessed=8 << 20, transcendentals=0),
+        name="prepare",
+    )(block, after, owner, cloud, *kept)
+
+
 def attend_kernel(
-    tok_ref, clear_ref, code_ref, gain_ref, scale_ref, we_ref, wqkv_ref, wo_ref, emb_ref, all_ref
+    scale_ref, tok_ref, mask_ref, code_ref, gain_ref, we_ref, wqkv_any, wo_any,
+    emb_ref, all_ref, wqkv_ref, wo_ref, sems,
 ):
+    copies = []
+    for c in range(4):
+        for part in range(3):
+            columns = pl.ds(1024 * part + 256 * c, 256)
+            copies.append(
+                pltpu.make_async_copy(
+                    wqkv_any.at[:, columns], wqkv_ref.at[:, columns], sems.at[3 * c + part]
+                )
+            )
+    copies.append(pltpu.make_async_copy(wo_any, wo_ref, sems.at[12]))
+    for copy in copies:
+        copy.start()
     encoded = mm(tok_ref[...], we_ref[...]).astype(BF).astype(F32)
     code = jnp.broadcast_to(code_ref[...][:, None, :], (32, 8, 1024)).reshape(256, 1024)
     state = encoded + code
@@ -125,23 +219,25 @@
     normed = (moved * lax.rsqrt(spread + 1e-05) * gain_ref[...].astype(F32)).astype(BF)
 
     seg = (iota((256, 256), 0) // 64 == iota((256, 256), 1) // 64).astype(BF)
-    qi = iota((256, 256), 0)
-    ki = iota((256, 256), 1)
-    mask = jnp.where(
-        (qi % 8 == ki % 8) & ((qi == ki) | (clear_ref[...] > 0.0)), jnp.float32(1), jnp.float32(0)
-    )
+    mask = mask_ref[...]
+    head = iota((1, 256), 1) // 64
     left = iota((256, 128), 1) < 64
     ones = jnp.ones((256, 128), BF)
     none = jnp.zeros((256, 128), BF)
     means = []
     for c in range(4):
-        span = slice(256 * c, 256 * c + 256)
+        scale = jnp.zeros((1, 256), F32)
+        for i in range(4):
+            scale = jnp.where(head == i, scale_ref[4 * c + i] * LOG2E, scale)
+        copies[3 * c].wait()
         queries = mm(normed, wqkv_ref[:, 256 * c : 256 * c + 256])
+        copies[3 * c + 1].wait()
         keys = mm(normed, wqkv_ref[:, 1024 + 256 * c : 1024 + 256 * c + 256])
+        copies[3 * c + 2].wait()
         values = mm(normed, wqkv_ref[:, 2048 + 256 * c : 2048 + 256 * c + 256]).astype(BF)
         q_sum = mm((queries * queries).astype(BF), seg)
         k_sum = mm((keys * keys).astype(BF), seg)
-        queries = (queries * (lax.rsqrt(q_sum + 1e-06) * (scale_ref[:, span] * LOG2E))).astype(BF)
+        queries = (queries * (lax.rsqrt(q_sum + 1e-06) * scale)).astype(BF)
         keys = (keys * lax.rsqrt(k_sum + 1e-06)).astype(BF)
         for pair in range(2):
             lanes = slice(128 * pair, 128 * pair + 128)
@@ -158,13 +254,14 @@
     mean = jnp.concatenate(means, axis=1)
     high = mean.astype(BF)
     low = (mean - high.astype(F32)).astype(BF)
+    copies[12].wait()
     update = mm(jnp.concatenate([high, low], axis=0), wo_ref[...])
     embedding = (state_mean + (update[0:8] + update[8:16])).astype(BF)
     emb_ref[...] = embedding
     all_ref[...] = jnp.broadcast_to(embedding[None], (32, 8, 1024))
 
 
-def attend(tokens, clear, code, gain, scale, w_embed, w_qkv, w_out):
+def attend(scale, tokens, mask, code, gain, w_embed, w_qkv, w_out):
     vmem = pl.BlockSpec(memory_space=pltpu.VMEM)
     return pl.pallas_call(
         attend_kernel,
@@ -172,23 +269,31 @@
             jax.ShapeDtypeStruct((8, 1024), BF),
             jax.ShapeDtypeStruct((32, 8, 1024), BF),
         ),
-        in_specs=[vmem] * 8,
+        in_specs=[pl.BlockSpec(memory_space=pltpu.SMEM)]
+        + [vmem] * 5
+        + [pl.BlockSpec(memory_space=pl.ANY)] * 2,
         out_specs=(vmem, vmem),
-        compiler_params=pltpu.CompilerParams(vmem_limit_bytes=40 << 20),
+        scratch_shapes=[
+            pltpu.VMEM((1024, 3072), BF),
+            pltpu.VMEM((1024, 1024), BF),
+            pltpu.SemaphoreType.DMA((13,)),
+        ],
+        compiler_params=pltpu.CompilerParams(vmem_limit_bytes=52 << 20),
         name="attend",
-    )(tokens, clear, code, gain, scale, w_embed, w_qkv, w_out)
-
-
-def contrast_kernel(scale_ref, emb_ref, all_ref, pos_ref, neg_ref, out_ref):
-    others = all_ref[...].astype(F32)
+    )(scale, tokens, mask, code, gain, w_embed, w_qkv, w_out)
+
+
+def contrast_kernel(scale_ref, block_ref, all_ref, pos_ref, neg_ref, out_ref):
+    others = all_ref[...].reshape(256, 1024).astype(F32)
     square = others * others
     high = square.astype(BF)
     low = (square - high.astype(F32)).astype(BF)
     ones = jnp.ones((8, 1024), BF)
     other_sum = mm_nt(ones, high) + mm_nt(ones, low)
-    anchors = emb_ref[...].astype(F32)
+    mine = all_ref[block_ref[0]]
+    anchors = mine.astype(F32)
     own_sum = jnp.sum(anchors * anchors, axis=1, keepdims=True)
-    similarity = mm_nt(emb_ref[...], all_ref[...])
+    similarity = mm_nt(mine, all_ref[...].reshape(256, 1024))
     similarity = similarity * lax.rsqrt(own_sum + 1e-06) * lax.rsqrt(other_sum + 1e-06)
     logits = similarity * scale_ref[0]
     member = iota((8, 256), 1)
@@ -203,16 +308,16 @@
     out_ref[...] = jnp.sum(jnp.where(diagonal, loss, 0.0), axis=0, keepdims=True)[:, 0:8]
 
 
-def contrast(scale, embedding, others, pos_ids, neg_ids):
+def contrast(scale, block, others, pos_ids, neg_ids):
     vmem = pl.BlockSpec(memory_space=pltpu.VMEM)
     return pl.pallas_call(
         contrast_kernel,
         out_shape=jax.ShapeDtypeStruct((1, 8), F32),
-        in_specs=[pl.BlockSpec(memory_space=pltpu.SMEM)] + [vmem] * 4,
+        in_specs=[pl.BlockSpec(memory_space=pltpu.SMEM)] * 2 + [vmem] * 3,
         out_specs=vmem,
         compiler_params=pltpu.CompilerParams(vmem_limit_bytes=16 << 20),
         name="contrast",
-    )(scale, embedding, others, pos_ids, neg_ids)
+    )(scale, block, others, pos_ids, neg_ids)
 
 
 def date_code(dates, width):
@@ -221,14 +326,6 @@
     angles = steps * np.exp(-2.0 * pair / width * np.log(10000.0))
     table = np.stack([np.sin(angles), np.cos(angles)], axis=-1).reshape(dates, width)
     return table.astype(np.float32)
-
-
-def slot_matrix(block_owner):
-    place = jnp.arange(PAR_DEV, dtype=I32)
-    same = (block_owner[:, None] == block_owner[None, :]) & (place[None, :] < place[:, None])
-    rank = jnp.sum(same.astype(I32), axis=1)
-    source = (block_owner * 16 + rank).reshape(8, 1, 8) + 4 * jnp.arange(4, dtype=I32)[None, :, None]
-    return (source.reshape(256, 1) == jnp.arange(512, dtype=I32)[None, :]).astype(BF)
 
 
 def per_device(
@@ -247,33 +344,28 @@
     pos_ids,
     neg_ids,
 ):
-    block = lax.axis_index("parcel")
+    block = lax.axis_index("parcel").reshape(1).astype(I32)
+    owner = owner.reshape(16, 128)
     pooled = pool_slots(
-        block.reshape(1).astype(I32),
-        tile_pixels,
-        owner.reshape(16, 128),
-        pix_count.reshape(16, 128),
-        w_pix1,
-        w_pix2,
+        block, tile_pixels, owner, pix_count.reshape(16, 128), w_pix1, w_pix2
     )
     arrived = lax.all_to_all(pooled, "parcel", split_axis=0, concat_axis=0, tiled=True)
-    pick = slot_matrix(lax.dynamic_slice_in_dim(owner[:, 0], block * PAR_DEV, PAR_DEV))
+    code = jnp.asarray(date_code(32, 1024))
+    pick, mask, code, w_embed = prepare(block, pooled, owner, cloud, code, w_embed)
     moving = mm(pick, arrived.reshape(512, 256)).astype(BF).reshape(8, 32, 256)
     tokens = lax.all_to_all(moving, "date", split_axis=0, concat_axis=0, tiled=True)
     embedding, copies = attend(
+        head_scale,
         tokens.reshape(256, 256),
-        (cloud.T == 0).astype(F32).reshape(1, 256),
-        jnp.asarray(date_code(32, 1024)),
+        mask,
+        code,
         norm_gain.reshape(1, 1024),
-        jnp.repeat(head_scale, 64).reshape(1, 1024),
         w_embed,
         w_qkv,
         w_out,
     )
     others = lax.all_to_all(copies, "parcel", split_axis=0, concat_axis=0, tiled=True)
-    loss = contrast(
-        logit_scale, embedding, others.reshape(256, 1024), pos_ids.reshape(8, 1), neg_ids
-    )
+    loss = contrast(logit_scale, block, others, pos_ids.reshape(8, 1), neg_ids)
     return (embedding, loss.reshape(8))
 
 

time: 82.7 us -> 77.8 us (0.941)
  local copies, waits for them, and re-layouts: 13 us -> 5.73 us
  Pallas kernels: 13.2 us -> 19.4 us
  waiting for transfers between devices: 31.5 us -> 29.6 us
  other arithmetic: 1.7 us -> 0 us
    unnamed x24 -> x16, local copies, waits for them, and re-layouts: 11 us -> 4.97 us
    pallas_call x1, Pallas kernels: 5.68 us -> 10.2 us  [attend(): pl.pallas_call(attend_kernel, out_shape=(jax.ShapeDtypeStruct((8, 1024),...]
    all_to_all x1, waiting for transfers between devices: 11 us -> 7.45 us  [per_device(): lax.all_to_all(pooled, 'parcel', split_axis=0, concat_axis=0, tiled=True)]
    all_to_all x1, waiting for transfers between devices: 3.78 us -> 5.45 us  [per_device(): lax.all_to_all(moving, 'date', split_axis=0, concat_axis=0, tiled=True)]
    pallas_call x1, Pallas kernels: 6.29 us -> 7.42 us  [pool_slots(): pl.pallas_call(pool_kernel, out_shape=jax.ShapeDtypeStruct((32, 16, 256),...]
  transfers between devices with their start and end apart: 3 -> 3, of which waited for: 3 -> 3; matrix products, arithmetic and copies ran while one was open for 5% -> 1% of each run, Pallas kernels for 0% -> 1%
where the time goes in v2:
time: 77.8 us; the launch traced here: 77.2 us
  waiting for transfers between devices  29.6 us (38%)
  starting transfers between devices  20.2 us (26%)
  Pallas kernels  19.4 us (25%)
  local copies, waits for them, and re-layouts  5.73 us (7%)
  between operations  1.35 us (2%)
  matrix products  0.89 us (1%)
    all_to_all x1, waiting for transfers between devices, per_device(): lax.all_to_all(copies, 'parcel', split_axis=0, concat_axis=0, tiled=True)  16.7 us
    all_to_all x1, starting transfers between devices, per_device(): lax.all_to_all(pooled, 'parcel', split_axis=0, concat_axis=0, tiled=True)  11.2 us
    pallas_call x1, Pallas kernels, attend(): pl.pallas_call(attend_kernel, out_shape=(jax.ShapeDtypeStruct((8, 1024),...  10.2 us
    all_to_all x1, waiting for transfers between devices, per_device(): lax.all_to_all(pooled, 'parcel', split_axis=0, concat_axis=0, tiled=True)  7.45 us
    pallas_call x1, Pallas kernels, pool_slots(): pl.pallas_call(pool_kernel, out_shape=jax.ShapeDtypeStruct((32, 16, 256),...  7.42 us
    all_to_all x1, waiting for transfers between devices, per_device(): lax.all_to_all(moving, 'date', split_axis=0, concat_axis=0, tiled=True)  5.45 us
    unnamed x16, local copies, waits for them, and re-layouts  4.97 us
    all_to_all x1, starting transfers between devices, per_device(): lax.all_to_all(copies, 'parcel', split_axis=0, concat_axis=0, tiled=True)  4.56 us
  transfers between devices with their start and end apart: 3, of which 3 were waited for; matrix products, arithmetic and copies ran while one was open for 1% of the time, Pallas kernels for 1%

profile of v2, /device:TPU:32, one launch (start us, length us, event | category | flops | bytes accessed | tf_op | source)
XLA Modules:
  0.0 77.2 jit_solution(13567293070321139404)
XLA Ops:
  0.6 7.4 %pool_slots.1.after = bf16[32,16,256]{2,1,0:T(8,128)(2,1)} custom-call(s32[1]{0:T(128)} %bitcast.tile_ref.block_ref, bf16[4,128,640]{2,1,0:T(8,128)(2,1)} %x_any.1, s32[16,128]{1,0:T(8,128)} %bitcast.11, s32[16,128]{1,0:T(8,128)} %bitcast.14, bf16[10,128]{1,0:T(8,128)(2,1)} %w1_any.1, bf16[128,128]{1,0:T(8,128)(2,1)} %w2_any.1), custom_call_target="tpu_custom_call" | custom-call | tf_op jit(solution)/shard_map/pool_slots/pallas_call | solution.py:115
  8.1 11.2 %all-to-all-start = ((bf16[32,16,256]{2,1,0:T(8,128)(2,1)}), bf16[32,16,256]{2,1,0:T(8,128)(2,1)S(1)}, u32[]{:S(2)}, u32[]{:S(2)}) async-start(bf16[32,16,256]{2,1,0:T(8,128)(2,1)} %pool_slots.1.after), calls=%async_computation | async-start | bytes 524288 | tf_op jit(solution)/shard_map/all_to_all | solution.py:352
  19.3 0.0 copy-start
  19.3 1.0 %copy-done = bf16[32,16,256]{2,1,0:T(8,128)(2,1)S(1)} copy-done((bf16[32,16,256]{2,1,0:T(8,128)(2,1)S(1)}, bf16[32,16,256]{2,1,0:T(8,128)(2,1)}, u32[]{:S(2)}) %copy-start) | copy-done | bytes 262168
  20.2 0.0 copy-start.1
  20.2 1.0 %copy-done.1 = bf16[256,1024]{1,0:T(8,128)(2,1)S(1)} copy-done((bf16[256,1024]{1,0:T(8,128)(2,1)S(1)}, bf16[256,1024]{1,0:T(8,128)(2,1)}, u32[]{:S(2)}) %copy-start.1) | copy-done | bytes 524312
  21.3 0.0 copy-start.2
  21.3 0.9 %copy-done.2 = f32[32,1024]{1,0:T(8,128)S(1)} copy-done((f32[32,1024]{1,0:T(8,128)S(1)}, f32[32,1024]{1,0:T(8,128)}, u32[]{:S(2)}) %copy-start.2) | copy-done | bytes 131096
  22.2 0.0 copy-start.3
  22.2 0.7 copy-done.3
  22.9 0.0 copy-start.4
  22.9 0.7 copy-done.4
  23.6 0.0 copy-start.7
  23.6 0.0 copy-start.5
  23.6 0.5 prepare.1
  24.1 7.5 %all-to-all-done = bf16[32,16,256]{2,1,0:T(8,128)(2,1)S(1)} async-done(((bf16[32,16,256]{2,1,0:T(8,128)(2,1)}), bf16[32,16,256]{2,1,0:T(8,128)(2,1)S(1)}, u32[]{:S(2)}, u32[]{:S(2)}) %all-to-all-start) | async-done | bytes 262176 | tf_op jit(solution)/shard_map/all_to_all | solution.py:352
  31.6 0.9 %convolution_convert_fusion = bf16[256,256]{1,0:T(8,128)(2,1)} fusion(bf16[256,512]{1,0:T(8,128)(2,1)S(1)} %get-tuple-element.8, bf16[512,256]{1,0:T(8,128)(2,1)S(1)} %bitcast.13), kind=kOutput, calls=%fused_computation | convolution fusion | flops 67174400 | bytes 655360 | tf_op jit(solution)/shard_map/dot_general | solution.py:23
  32.4 4.5 %all-to-all-start.1 = ((bf16[8,32,256]{2,1,0:T(8,128)(2,1)}), bf16[8,32,256]{2,1,0:T(8,128)(2,1)S(1)}, u32[]{:S(2)}, u32[]{:S(2)}) async-start(bf16[8,32,256]{2,1,0:T(8,128)(2,1)} %bitcast.4), calls=%async_computation.1 | async-start | bytes 262144 | tf_op jit(solution)/shard_map/all_to_all | solution.py:356
  36.9 0.7 reshape.37.gain_ref
  37.6 5.4 %all-to-all-done.1 = bf16[8,32,256]{2,1,0:T(8,128)(2,1)S(1)} async-done(((bf16[8,32,256]{2,1,0:T(8,128)(2,1)}), bf16[8,32,256]{2,1,0:T(8,128)(2,1)S(1)}, u32[]{:S(2)}, u32[]{:S(2)}) %all-to-all-start.1) | async-done | bytes 131104 | tf_op jit(solution)/shard_map/all_to_all | solution.py:356
  43.1 0.0 copy-start.6
  43.1 0.7 copy-done.6
  43.7 10.2 %attend.1 = (bf16[8,1024]{1,0:T(8,128)(2,1)}, bf16[32,8,1024]{2,1,0:T(8,128)(2,1)}) custom-call(f32[16]{0:T(128)S(1)} %copy-done.6, bf16[256,256]{1,0:T(8,128)(2,1)S(1)} %bitcast.10, f32[256,256]{1,0:T(8,128)S(1)} %get-tuple-element.9.mask_ref, f32[32,1024]{1,0:T(8,128)S(1)} %get-tuple-element.10.code_ref, bf16[1,1024]{1,0:T(2,128)(2,1)S(1)} %reshape.37.gain_ref, ...), custom_call_target="tpu_custom_call" | custom-call | tf_op jit(solution)/shard_map/attend/pallas_call | solution.py:266
  53.9 4.6 %all-to-all-start.2 = ((bf16[32,8,1024]{2,1,0:T(8,128)(2,1)}), bf16[32,8,1024]{2,1,0:T(8,128)(2,1)S(1)}, u32[]{:S(2)}, u32[]{:S(2)}) async-start(bf16[32,8,1024]{2,1,0:T(8,128)(2,1)} %get-tuple-element.13), calls=%async_computation.2 | async-start | bytes 1048576 | tf_op jit(solution)/shard_map/all_to_all | solution.py:367
  58.5 0.0 copy-done.7
  58.5 0.1 copy.17.pos_ref
  59.2 16.7 %all-to-all-done.2.all_ref = bf16[32,8,1024]{2,1,0:T(8,128)(2,1)S(1)} async-done(((bf16[32,8,1024]{2,1,0:T(8,128)(2,1)}), bf16[32,8,1024]{2,1,0:T(8,128)(2,1)S(1)}, u32[]{:S(2)}, u32[]{:S(2)}) %all-to-all-start.2) | async-done | bytes 524320 | tf_op jit(solution)/shard_map/all_to_all | solution.py:367
  75.9 0.0 copy-done.5
  75.9 1.3 %contrast.1 = f32[1,8]{1,0:T(1,128)} custom-call(f32[1]{0:T(128)S(6)} %copy.18.scale_ref, s32[1]{0:T(128)} %bitcast.tile_ref.block_ref, bf16[32,8,1024]{2,1,0:T(8,128)(2,1)S(1)} %all-to-all-done.2.all_ref, s32[8,1]{1,0:T(8,128)S(1)} %copy.17.pos_ref, s32[8,128]{1,0:T(8,128)S(1)} %copy-done.5), custom_call_target="tpu_custom_call" | custom-call | tf_op jit(solution)/shard_map/contrast/pallas_call | solution.py:313
Async XLA Ops:
  8.1 23.5 %all-to-all-start = ((bf16[32,16,256]{2,1,0:T(8,128)(2,1)}), bf16[32,16,256]{2,1,0:T(8,128)(2,1)S(1)}, u32[]{:S(2)}, u32[]{:S(2)}) async-start(bf16[32,16,256]{2,1,0:T(8,128)(2,1)} %pool_slots.1.after), calls=%async_computation | async-start | bytes 524288 | tf_op jit(solution)/shard_map/all_to_all | solution.py:352
  19.3 1.0 %copy-start = (bf16[32,16,256]{2,1,0:T(8,128)(2,1)S(1)}, bf16[32,16,256]{2,1,0:T(8,128)(2,1)}, u32[]{:S(2)}) copy-start(bf16[32,16,256]{2,1,0:T(8,128)(2,1)} %pool_slots.1.after) | copy-start | bytes 786436
  20.2 1.0 %copy-start.1 = (bf16[256,1024]{1,0:T(8,128)(2,1)S(1)}, bf16[256,1024]{1,0:T(8,128)(2,1)}, u32[]{:S(2)}) copy-start(bf16[256,1024]{1,0:T(8,128)(2,1)} %we_any.1) | copy-start | bytes 1572868
  21.3 0.9 %copy-start.2 = (f32[32,1024]{1,0:T(8,128)S(1)}, f32[32,1024]{1,0:T(8,128)}, u32[]{:S(2)}) copy-start(f32[32,1024]{1,0:T(8,128)} %constant.6.clone.code_any) | copy-start | bytes 393220
  22.2 0.7 copy-start.3
  22.9 0.7 copy-start.4
  23.6 34.9 %copy-start.7 = (s32[8]{0:T(128)S(1)}, s32[8]{0:T(128)}, u32[]{:S(2)}) copy-start(s32[8]{0:T(128)} %param.27) | copy-start | bytes 100
  23.6 52.4 %copy-start.5 = (s32[8,128]{1,0:T(8,128)S(1)}, s32[8,128]{1,0:T(8,128)}, u32[]{:S(2)}) copy-start(s32[8,128]{1,0:T(8,128)} %neg_ref.1) | copy-start | bytes 12292
  32.4 10.6 %all-to-all-start.1 = ((bf16[8,32,256]{2,1,0:T(8,128)(2,1)}), bf16[8,32,256]{2,1,0:T(8,128)(2,1)S(1)}, u32[]{:S(2)}, u32[]{:S(2)}) async-start(bf16[8,32,256]{2,1,0:T(8,128)(2,1)} %bitcast.4), calls=%async_computation.1 | async-start | bytes 262144 | tf_op jit(solution)/shard_map/all_to_all | solution.py:356
  43.1 0.7 copy-start.6
  53.9 22.0 %all-to-all-start.2 = ((bf16[32,8,1024]{2,1,0:T(8,128)(2,1)}), bf16[32,8,1024]{2,1,0:T(8,128)(2,1)S(1)}, u32[]{:S(2)}, u32[]{:S(2)}) async-start(bf16[32,8,1024]{2,1,0:T(8,128)(2,1)} %get-tuple-element.13), calls=%async_computation.2 | async-start | bytes 1048576 | tf_op jit(solution)/shard_map/all_to_all | solution.py:367

commit v3 on v2

--- a/solution.py
+++ b/solution.py
@@ -133,12 +133,13 @@
 
 
 def prepare_kernel(
-    block_ref, after, own_any, cloud_any, code_any, we_any,
-    pick_ref, mask_ref, code_ref, we_ref, own_ref, cloud_ref, sems,
+    block_ref, scale_ref, after, own_any, cloud_any, gain_any, code_any, we_any,
+    pick_ref, mask_ref, row_ref, code_ref, we_ref, own_ref, cloud_ref, gain_ref, sems,
 ):
     pairs = [
         (own_any, own_ref),
         (cloud_any, cloud_ref),
+        (gain_any, gain_ref),
         (we_any, we_ref),
         (code_any, code_ref),
     ]
@@ -167,77 +168,111 @@
     qi = iota((256, 256), 0)
     ki = iota((256, 256), 1)
     mask_ref[...] = jnp.where((qi % 8 == ki % 8) & ((qi == ki) | (cloudy == 0.0)), 1.0, 0.0)
-    for copy in copies[2:]:
+    head = iota((1, 1024), 1) // 64
+    scale = jnp.zeros((1, 1024), F32)
+    for i in range(16):
+        scale = jnp.where(head == i, scale_ref[i] * LOG2E, scale)
+    copies[2].wait()
+    gain = gain_ref[...].astype(F32)
+    gain = jnp.concatenate([gain[i : i + 1] for i in range(8)], axis=1)
+    row_ref[...] = jnp.where(iota((8, 1024), 0) == 0, scale, gain)
+    for copy in copies[3:]:
         copy.wait()
 
 
-def prepare(block, after, owner, cloud, code, w_embed):
-    kept = (code, w_embed)
+def prepare(block, scale, after, owner, cloud, gain, code, w_embed):
     return pl.pallas_call(
         prepare_kernel,
         out_shape=(
             jax.ShapeDtypeStruct((256, 512), BF),
             jax.ShapeDtypeStruct((256, 256), F32),
-        )
-        + tuple(jax.ShapeDtypeStruct(a.shape, a.dtype) for a in kept),
-        in_specs=[pl.BlockSpec(memory_space=pltpu.SMEM)] + [pl.BlockSpec(memory_space=pl.ANY)] * 5,
-        out_specs=(pl.BlockSpec(memory_space=pltpu.VMEM),) * 4,
+            jax.ShapeDtypeStruct((8, 1024), F32),
+            jax.ShapeDtypeStruct((32, 1024), F32),
+            jax.ShapeDtypeStruct((256, 1024), BF),
+        ),
+        in_specs=[pl.BlockSpec(memory_space=pltpu.SMEM)] * 2
+        + [pl.BlockSpec(memory_space=pl.ANY)] * 6,
+        out_specs=(pl.BlockSpec(memory_space=pltpu.VMEM),) * 5,
         scratch_shapes=[
             pltpu.VMEM((16, 128), I32),
             pltpu.VMEM((8, 32), I32),
-            pltpu.SemaphoreType.DMA((4,)),
+            pltpu.VMEM((8, 128), BF),
+            pltpu.SemaphoreType.DMA((5,)),
         ],
         compiler_params=pltpu.CompilerParams(vmem_limit_bytes=48 << 20),
         cost_estimate=pl.CostEstimate(flops=0, bytes_accessed=8 << 20, transcendentals=0),
         name="prepare",
-    )(block, after, owner, cloud, *kept)
+    )(block, scale, after, owner, cloud, gain, code, w_embed)
+
+
+def pick_kernel(pick_ref, rows_ref, out_ref):
+    rows = rows_ref[...].reshape(512, 256)
+    out_ref[...] = mm(pick_ref[...], rows).astype(BF).reshape(8, 32, 256)
+
+
+def pick_rows(pick, rows):
+    vmem = pl.BlockSpec(memory_space=pltpu.VMEM)
+    return pl.pallas_call(
+        pick_kernel,
+        out_shape=jax.ShapeDtypeStruct((8, 32, 256), BF),
+        in_specs=[vmem] * 2,
+        out_specs=vmem,
+        compiler_params=pltpu.CompilerParams(vmem_limit_bytes=16 << 20),
+        name="pick_rows",
+    )(pick, rows)
 
 
 def attend_kernel(
-    scale_ref, tok_ref, mask_ref, code_ref, gain_ref, we_ref, wqkv_any, wo_any,
-    emb_ref, all_ref, wqkv_ref, wo_ref, sems,
+    tok_ref, mask_ref, row_ref, code_ref, we_ref, wqkv_any, wo_any,
+    emb_ref, all_ref, w_ref, wo_ref, sems,
 ):
-    copies = []
-    for c in range(4):
-        for part in range(3):
-            columns = pl.ds(1024 * part + 256 * c, 256)
-            copies.append(
-                pltpu.make_async_copy(
-                    wqkv_any.at[:, columns], wqkv_ref.at[:, columns], sems.at[3 * c + part]
-                )
+    chunks = [
+        [
+            pltpu.make_async_copy(
+                wqkv_any.at[:, 1024 * part + 256 * c : 1024 * part + 256 * c + 256],
+                w_ref.at[c, :, 256 * part : 256 * part + 256],
+                sems.at[3 * c + part],
             )
-    copies.append(pltpu.make_async_copy(wo_any, wo_ref, sems.at[12]))
-    for copy in copies:
-        copy.start()
+            for part in range(3)
+        ]
+        for c in range(4)
+    ]
+    chunks.append([pltpu.make_async_copy(wo_any, wo_ref, sems.at[12])])
+
+    def start(number):
+        for copy in chunks[number]:
+            copy.start()
+
+    start(0)
     encoded = mm(tok_ref[...], we_ref[...]).astype(BF).astype(F32)
     code = jnp.broadcast_to(code_ref[...][:, None, :], (32, 8, 1024)).reshape(256, 1024)
     state = encoded + code
+    start(1)
     state_mean = jnp.mean(state.reshape(32, 8, 1024), axis=0)
     center = jnp.mean(state, axis=1, keepdims=True)
     moved = state - center
     spread = jnp.mean(moved * moved, axis=1, keepdims=True)
-    normed = (moved * lax.rsqrt(spread + 1e-05) * gain_ref[...].astype(F32)).astype(BF)
+    normed = (moved * lax.rsqrt(spread + 1e-05) * row_ref[1:2, :]).astype(BF)
 
     seg = (iota((256, 256), 0) // 64 == iota((256, 256), 1) // 64).astype(BF)
     mask = mask_ref[...]
-    head = iota((1, 256), 1) // 64
     left = iota((256, 128), 1) < 64
     ones = jnp.ones((256, 128), BF)
     none = jnp.zeros((256, 128), BF)
     means = []
     for c in range(4):
-        scale = jnp.zeros((1, 256), F32)
-        for i in range(4):
-            scale = jnp.where(head == i, scale_ref[4 * c + i] * LOG2E, scale)
-        copies[3 * c].wait()
-        queries = mm(normed, wqkv_ref[:, 256 * c : 256 * c + 256])
-        copies[3 * c + 1].wait()
-        keys = mm(normed, wqkv_ref[:, 1024 + 256 * c : 1024 + 256 * c + 256])
-        copies[3 * c + 2].wait()
-        values = mm(normed, wqkv_ref[:, 2048 + 256 * c : 2048 + 256 * c + 256]).astype(BF)
+        for copy in chunks[c]:
+            copy.wait()
+        if c < 3:
+            start(c + 2)
+        queries = mm(normed, w_ref[c, :, 0:256])
+        keys = mm(normed, w_ref[c, :, 256:512])
+        values = mm(normed, w_ref[c, :, 512:768]).astype(BF)
         q_sum = mm((queries * queries).astype(BF), seg)
         k_sum = mm((keys * keys).astype(BF), seg)
-        queries = (queries * (lax.rsqrt(q_sum + 1e-06) * scale)).astype(BF)
+        queries = (queries * (
+            lax.rsqrt(q_sum + 1e-06) * row_ref[0:1, 256 * c : 256 * c + 256]
+        )).astype(BF)
         keys = (keys * lax.rsqrt(k_sum + 1e-06)).astype(BF)
         for pair in range(2):
             lanes = slice(128 * pair, 128 * pair + 128)
@@ -254,14 +289,14 @@
     mean = jnp.concatenate(means, axis=1)
     high = mean.astype(BF)
     low = (mean - high.astype(F32)).astype(BF)
-    copies[12].wait()
+    chunks[4][0].wait()
     update = mm(jnp.concatenate([high, low], axis=0), wo_ref[...])
     embedding = (state_mean + (update[0:8] + update[8:16])).astype(BF)
     emb_ref[...] = embedding
     all_ref[...] = jnp.broadcast_to(embedding[None], (32, 8, 1024))
 
 
-def attend(scale, tokens, mask, code, gain, w_embed, w_qkv, w_out):
+def attend(tokens, mask, rows, code, w_embed, w_qkv, w_out):
     vmem = pl.BlockSpec(memory_space=pltpu.VMEM)
     return pl.pallas_call(
         attend_kernel,
@@ -269,18 +304,16 @@
             jax.ShapeDtypeStruct((8, 1024), BF),
             jax.ShapeDtypeStruct((32, 8, 1024), BF),
         ),
-        in_specs=[pl.BlockSpec(memory_space=pltpu.SMEM)]
-        + [vmem] * 5
-        + [pl.BlockSpec(memory_space=pl.ANY)] * 2,
+        in_specs=[vmem] * 5 + [pl.BlockSpec(memory_space=pl.ANY)] * 2,
         out_specs=(vmem, vmem),
         scratch_shapes=[
-            pltpu.VMEM((1024, 3072), BF),
+            pltpu.VMEM((4, 1024, 768), BF),
             pltpu.VMEM((1024, 1024), BF),
             pltpu.SemaphoreType.DMA((13,)),
         ],
         compiler_params=pltpu.CompilerParams(vmem_limit_bytes=52 << 20),
         name="attend",
-    )(scale, tokens, mask, code, gain, w_embed, w_qkv, w_out)
+    )(tokens, mask, rows, code, w_embed, w_qkv, w_out)
 
 
 def contrast_kernel(scale_ref, block_ref, all_ref, pos_ref, neg_ref, out_ref):
@@ -351,15 +384,16 @@
     )
     arrived = lax.all_to_all(pooled, "parcel", split_axis=0, concat_axis=0, tiled=True)
     code = jnp.asarray(date_code(32, 1024))
-    pick, mask, code, w_embed = prepare(block, pooled, owner, cloud, code, w_embed)
-    moving = mm(pick, arrived.reshape(512, 256)).astype(BF).reshape(8, 32, 256)
+    pick, mask, rows, code, w_embed = prepare(
+        block, head_scale, pooled, owner, cloud, norm_gain.reshape(8, 128), code, w_embed
+    )
+    moving = pick_rows(pick, arrived)
     tokens = lax.all_to_all(moving, "date", split_axis=0, concat_axis=0, tiled=True)
     embedding, copies = attend(
-        head_scale,
         tokens.reshape(256, 256),
         mask,
+        rows,
         code,
-        norm_gain.reshape(1, 1024),
         w_embed,
         w_qkv,
         w_out,

time: 77.8 us -> 73.6 us (0.946)
  blocking collectives: 0 us -> 10.4 us
  waiting for transfers between devices: 29.6 us -> 22.2 us
  starting transfers between devices: 20.2 us -> 15.8 us
  Pallas kernels: 19.4 us -> 17.6 us
  matrix products: 0.89 us -> 0 us
    all_to_all x0 -> x1, blocking collectives: none -> 10.4 us  [per_device(): lax.all_to_all(moving, 'date', split_axis=0, concat_axis=0, tiled=True)]
    all_to_all x1 -> x0, waiting for transfers between devices: 5.45 us -> none  [per_device(): lax.all_to_all(moving, 'date', split_axis=0, concat_axis=0, tiled=True)]
    all_to_all x1 -> x0, starting transfers between devices: 4.48 us -> none  [per_device(): lax.all_to_all(moving, 'date', split_axis=0, concat_axis=0, tiled=True)]
    pallas_call x1, Pallas kernels: 10.2 us -> 7.58 us  [attend(): pl.pallas_call(attend_kernel, out_shape=(jax.ShapeDtypeStruct((8, 1024),...]
    all_to_all x1, waiting for transfers between devices: 7.45 us -> 5.53 us  [per_device(): lax.all_to_all(pooled, 'parcel', split_axis=0, concat_axis=0, tiled=True)]
    dot_general x1 -> x0, matrix products: 0.89 us -> none  [mm(): return jnp.dot(left, right, preferred_element_type=F32)]
    unnamed x16 -> x18, local copies, waits for them, and re-layouts: 4.97 us -> 5.65 us
  transfers between devices with their start and end apart: 3 -> 2, of which waited for: 3 -> 2; matrix products, arithmetic and copies ran while one was open for 1% -> 0% of each run, Pallas kernels for 1% -> 1%
where the time goes in v3:
time: 73.6 us; the launch traced here: 73.1 us
  waiting for transfers between devices  22.2 us (30%)
  Pallas kernels  17.6 us (24%)
  starting transfers between devices  15.8 us (21%)
  blocking collectives  10.4 us (14%)
  local copies, waits for them, and re-layouts  5.73 us (8%)
  between operations  1.36 us (2%)
    all_to_all x1, waiting for transfers between devices, per_device(): lax.all_to_all(copies, 'parcel', split_axis=0, concat_axis=0, tiled=True)  16.7 us
    all_to_all x1, starting transfers between devices, per_device(): lax.all_to_all(pooled, 'parcel', split_axis=0, concat_axis=0, tiled=True)  11.2 us
    all_to_all x1, blocking collectives, per_device(): lax.all_to_all(moving, 'date', split_axis=0, concat_axis=0, tiled=True)  10.4 us
    pallas_call x1, Pallas kernels, attend(): pl.pallas_call(attend_kernel, out_shape=(jax.ShapeDtypeStruct((8, 1024),...  7.58 us
    pallas_call x1, Pallas kernels, pool_slots(): pl.pallas_call(pool_kernel, out_shape=jax.ShapeDtypeStruct((32, 16, 256),...  7.43 us
    unnamed x18, local copies, waits for them, and re-layouts  5.65 us
    all_to_all x1, waiting for transfers between devices, per_device(): lax.all_to_all(pooled, 'parcel', split_axis=0, concat_axis=0, tiled=True)  5.53 us
    all_to_all x1, starting transfers between devices, per_device(): lax.all_to_all(copies, 'parcel', split_axis=0, concat_axis=0, tiled=True)  4.57 us
  transfers between devices with their start and end apart: 2, of which 2 were waited for; matrix products, arithmetic and copies ran while one was open for 0% of the time, Pallas kernels for 1%

profile of v3, /device:TPU:32, one launch (start us, length us, event | category | flops | bytes accessed | tf_op | source)
XLA Modules:
  0.0 73.1 jit_solution(14629269678076518087)
XLA Ops:
  0.6 7.4 %pool_slots.1.after = bf16[32,16,256]{2,1,0:T(8,128)(2,1)} custom-call(s32[1]{0:T(128)} %bitcast.tile_ref.block_ref, bf16[4,128,640]{2,1,0:T(8,128)(2,1)} %x_any.1, s32[16,128]{1,0:T(8,128)} %bitcast.8, s32[16,128]{1,0:T(8,128)} %bitcast.11, bf16[10,128]{1,0:T(8,128)(2,1)} %w1_any.1, bf16[128,128]{1,0:T(8,128)(2,1)} %w2_any.1), custom_call_target="tpu_custom_call" | custom-call | tf_op jit(solution)/shard_map/pool_slots/pallas_call | solution.py:115
  8.1 11.2 %all-to-all-start = ((bf16[32,16,256]{2,1,0:T(8,128)(2,1)}), bf16[32,16,256]{2,1,0:T(8,128)(2,1)S(1)}, u32[]{:S(2)}, u32[]{:S(2)}) async-start(bf16[32,16,256]{2,1,0:T(8,128)(2,1)} %pool_slots.1.after), calls=%async_computation | async-start | bytes 524288 | tf_op jit(solution)/shard_map/all_to_all | solution.py:385
  19.3 0.0 copy-start.8
  19.3 0.0 copy-start
  19.3 1.0 %copy-done = bf16[32,16,256]{2,1,0:T(8,128)(2,1)S(1)} copy-done((bf16[32,16,256]{2,1,0:T(8,128)(2,1)S(1)}, bf16[32,16,256]{2,1,0:T(8,128)(2,1)}, u32[]{:S(2)}) %copy-start) | copy-done | bytes 262168
  20.3 0.0 copy-start.1
  20.3 1.0 %copy-done.1 = bf16[256,1024]{1,0:T(8,128)(2,1)S(1)} copy-done((bf16[256,1024]{1,0:T(8,128)(2,1)S(1)}, bf16[256,1024]{1,0:T(8,128)(2,1)}, u32[]{:S(2)}) %copy-start.1) | copy-done | bytes 524312
  21.3 0.0 copy-start.2
  21.3 0.9 %copy-done.2 = f32[32,1024]{1,0:T(8,128)S(1)} copy-done((f32[32,1024]{1,0:T(8,128)S(1)}, f32[32,1024]{1,0:T(8,128)}, u32[]{:S(2)}) %copy-start.2) | copy-done | bytes 131096
  22.2 0.0 copy-start.3
  22.2 0.7 copy-done.3
  22.9 0.0 copy-start.4
  22.9 0.7 copy-done.4
  23.6 0.0 copy-start.6
  23.6 0.7 copy-done.6
  24.3 0.0 copy-start.7
  24.3 0.7 copy-done.7
  24.9 0.0 copy-start.5
  24.9 1.1 %prepare.1 = (bf16[256,512]{1,0:T(8,128)(2,1)S(1)}, f32[256,256]{1,0:T(8,128)S(1)}, f32[8,1024]{1,0:T(8,128)S(1)}, f32[32,1024]{1,0:T(8,128)S(1)}, bf16[256,1024]{1,0:T(8,128)(2,1)S(1)}) custom-call(s32[1]{0:T(128)} %bitcast.tile_ref.block_ref, f32[16]{0:T(128)S(1)} %copy-done.7, bf16[32,16,256]{2,1,0:T(8,128)(2,1)S(1)} %copy-done, s32[16,128]{1,0:T(8,128)S(1)} %bitcast.9, ...), custom_call_target="tpu_custom_call" | custom-call | bytes 8388608 | tf_op jit(solution)/shard_map/prepare/pallas_call | solution.py:184
  26.0 5.5 %all-to-all-done.rows_ref = bf16[32,16,256]{2,1,0:T(8,128)(2,1)S(1)} async-done(((bf16[32,16,256]{2,1,0:T(8,128)(2,1)}), bf16[32,16,256]{2,1,0:T(8,128)(2,1)S(1)}, u32[]{:S(2)}, u32[]{:S(2)}) %all-to-all-start) | async-done | bytes 262176 | tf_op jit(solution)/shard_map/all_to_all | solution.py:385
  31.6 0.2 pick_rows.1
  31.8 10.4 %all_to_all.15 = bf16[8,32,256]{2,1,0:T(8,128)(2,1)S(1)} all-to-all(bf16[8,32,256]{2,1,0:T(8,128)(2,1)S(1)} %pick_rows.1), channel_id=1, replica_groups=mesh['date'=8,'parcel'=32] {'date'}, dimensions={0} | all-to-all | bytes 262144 | tf_op jit(solution)/shard_map/all_to_all | solution.py:391
  42.2 7.6 %attend.1 = (bf16[8,1024]{1,0:T(8,128)(2,1)}, bf16[32,8,1024]{2,1,0:T(8,128)(2,1)}) custom-call(bf16[256,256]{1,0:T(8,128)(2,1)S(1)} %bitcast.7, f32[256,256]{1,0:T(8,128)S(1)} %get-tuple-element.10.mask_ref, f32[8,1024]{1,0:T(8,128)S(1)} %get-tuple-element.11.row_ref, f32[32,1024]{1,0:T(8,128)S(1)} %get-tuple-element.12.code_ref, ...), custom_call_target="tpu_custom_call" | custom-call | tf_op jit(solution)/shard_map/attend/pallas_call | solution.py:301
  49.8 4.6 %all-to-all-start.2 = ((bf16[32,8,1024]{2,1,0:T(8,128)(2,1)}), bf16[32,8,1024]{2,1,0:T(8,128)(2,1)S(1)}, u32[]{:S(2)}, u32[]{:S(2)}) async-start(bf16[32,8,1024]{2,1,0:T(8,128)(2,1)} %get-tuple-element.15), calls=%async_computation.2 | async-start | bytes 1048576 | tf_op jit(solution)/shard_map/all_to_all | solution.py:401
  55.0 0.0 copy-done.8
  55.0 0.1 copy.17.pos_ref
  55.1 16.7 %all-to-all-done.2.all_ref = bf16[32,8,1024]{2,1,0:T(8,128)(2,1)S(1)} async-done(((bf16[32,8,1024]{2,1,0:T(8,128)(2,1)}), bf16[32,8,1024]{2,1,0:T(8,128)(2,1)S(1)}, u32[]{:S(2)}, u32[]{:S(2)}) %all-to-all-start.2) | async-done | bytes 524320 | tf_op jit(solution)/shard_map/all_to_all | solution.py:401
  71.8 0.0 copy-done.5
  71.8 1.3 %contrast.1 = f32[1,8]{1,0:T(1,128)} custom-call(f32[1]{0:T(128)S(6)} %copy.18.scale_ref, s32[1]{0:T(128)} %bitcast.tile_ref.block_ref, bf16[32,8,1024]{2,1,0:T(8,128)(2,1)S(1)} %all-to-all-done.2.all_ref, s32[8,1]{1,0:T(8,128)S(1)} %copy.17.pos_ref, s32[8,128]{1,0:T(8,128)S(1)} %copy-done.5), custom_call_target="tpu_custom_call" | custom-call | tf_op jit(solution)/shard_map/contrast/pallas_call | solution.py:346
Async XLA Ops:
  8.1 23.5 %all-to-all-start = ((bf16[32,16,256]{2,1,0:T(8,128)(2,1)}), bf16[32,16,256]{2,1,0:T(8,128)(2,1)S(1)}, u32[]{:S(2)}, u32[]{:S(2)}) async-start(bf16[32,16,256]{2,1,0:T(8,128)(2,1)} %pool_slots.1.after), calls=%async_computation | async-start | bytes 524288 | tf_op jit(solution)/shard_map/all_to_all | solution.py:385
  19.3 35.7 %copy-start.8 = (s32[8]{0:T(128)S(1)}, s32[8]{0:T(128)}, u32[]{:S(2)}) copy-start(s32[8]{0:T(128)} %param.27) | copy-start | bytes 100
  19.3 1.0 %copy-start = (bf16[32,16,256]{2,1,0:T(8,128)(2,1)S(1)}, bf16[32,16,256]{2,1,0:T(8,128)(2,1)}, u32[]{:S(2)}) copy-start(bf16[32,16,256]{2,1,0:T(8,128)(2,1)} %pool_slots.1.after) | copy-start | bytes 786436
  20.3 1.0 %copy-start.1 = (bf16[256,1024]{1,0:T(8,128)(2,1)S(1)}, bf16[256,1024]{1,0:T(8,128)(2,1)}, u32[]{:S(2)}) copy-start(bf16[256,1024]{1,0:T(8,128)(2,1)} %we_any.1) | copy-start | bytes 1572868
  21.3 0.9 %copy-start.2 = (f32[32,1024]{1,0:T(8,128)S(1)}, f32[32,1024]{1,0:T(8,128)}, u32[]{:S(2)}) copy-start(f32[32,1024]{1,0:T(8,128)} %constant.6.clone.code_any) | copy-start | bytes 393220
  22.2 0.7 copy-start.3
  22.9 0.7 copy-start.4
  23.6 0.7 copy-start.6
  24.3 0.7 copy-start.7
  24.9 46.9 %copy-start.5 = (s32[8,128]{1,0:T(8,128)S(1)}, s32[8,128]{1,0:T(8,128)}, u32[]{:S(2)}) copy-start(s32[8,128]{1,0:T(8,128)} %neg_ref.1) | copy-start | bytes 12292
  49.8 22.0 %all-to-all-start.2 = ((bf16[32,8,1024]{2,1,0:T(8,128)(2,1)}), bf16[32,8,1024]{2,1,0:T(8,128)(2,1)S(1)}, u32[]{:S(2)}, u32[]{:S(2)}) async-start(bf16[32,8,1024]{2,1,0:T(8,128)(2,1)} %get-tuple-element.15), calls=%async_computation.2 | async-start | bytes 1048576 | tf_op jit(solution)/shard_map/all_to_all | solution.py:401

commit v4 on v3

--- a/solution.py
+++ b/solution.py
@@ -32,20 +32,47 @@
 
 
 def pool_kernel(
-    tile_ref, x_any, own_any, cnt_any, w1_any, w2_any, out_ref,
+    tile_ref, x_any, own_any, cnt_any, w1_any, w2_any, out_ref, done_ref,
     x_ref, own_ref, cnt_ref, w1_ref, w2_ref, w1s, ps, sems,
 ):
-    pairs = [(own_any, own_ref), (cnt_any, cnt_ref), (w1_any, w1_ref), (w2_any, w2_ref), (x_any, x_ref)]
+    rows = 4 * 128
+    pairs = [(w1_any, w1_ref), (own_any, own_ref), (cnt_any, cnt_ref), (w2_any, w2_ref), (x_any, x_ref)]
     copies = [pltpu.make_async_copy(a, b, sems.at[i]) for i, (a, b) in enumerate(pairs)]
     for copy in copies:
         copy.start()
-    copies[0].wait()
-    copies[1].wait()
-    rows = 4 * 128
-    match = own_ref[...] == tile_ref[0]
+    done_ref[0] = tile_ref[0]
+    w1s[...] = jnp.zeros((32, 256, 256), BF)
     li = iota((128, 128), 0)
     lj = iota((128, 128), 1)
     before = ((li < lj) & ((li // 64) == (lj // 64))).astype(BF)
+    to_all = ((iota((128, 640), 1) % 10) == iota((128, 640), 0)).astype(BF)
+    channel = (iota((640, 16), 0) % 10 == iota((640, 16), 1)).astype(BF)
+    po = iota((256, 256), 0)
+    pi = iota((256, 256), 1)
+    order = ((po // 16 == pi // 4 % 16) & (po // 4 % 4 == pi // 64) & (po % 4 == pi % 4)).astype(BF)
+
+    copies[0].wait()
+    w1 = jnp.concatenate([w1_ref[...].astype(F32), jnp.zeros((6, 128), F32)], axis=0)
+    tiled = mm(channel, w1.astype(BF))
+    windows = []
+    for j in range(SETS // 2):
+        low = 20 * j
+        start = low // 128 * 128
+        windows.append((start, 256 if low + 20 > start + 128 else 128))
+        top = low // 16 * 16
+        end = -(-(low + 20) // 16) * 16
+        part = tiled[top:end]
+        row = iota((end - top, 128), 0) + top
+        w1s[j, top - start : end - start, 0:128] = jnp.where(
+            (row >= low) & (row < low + 10), part, 0.0
+        ).astype(BF)
+        w1s[j, top - start : end - start, 128:256] = jnp.where(
+            (row >= low + 10) & (row < low + 20), part, 0.0
+        ).astype(BF)
+
+    copies[1].wait()
+    copies[2].wait()
+    match = own_ref[...] == tile_ref[0]
     rank = mm(match.astype(F32).astype(BF), before)
     code = jnp.where(match, rank.astype(I32), -1)
     sub = iota((16, 8, 128), 1)
@@ -54,24 +81,8 @@
     amount = jnp.where(hit, cnt_ref[...][:, None, :], 0).reshape(128, 128)
     counts = mm(amount.astype(F32).astype(BF), jnp.ones((128, 128), BF))
 
-    copies[2].wait()
-    channel = (iota((640, 16), 0) % 10 == iota((640, 16), 1)).astype(BF)
-    w1 = jnp.concatenate([w1_ref[...].astype(F32), jnp.zeros((6, 128), F32)], axis=0)
-    tiled = mm(channel, w1.astype(BF))
-    windows = []
-    for j in range(SETS // 2):
-        low = 20 * j
-        start = low // 128 * 128
-        depth = 256 if low + 20 > start + 128 else 128
-        windows.append((start, depth))
-        part = tiled[start : start + depth]
-        row = iota((depth, 128), 0) + start
-        w1s[j, 0:depth, 0:128] = jnp.where((row >= low) & (row < low + 10), part, 0.0).astype(BF)
-        w1s[j, 0:depth, 128:256] = jnp.where(
-            (row >= low + 10) & (row < low + 20), part, 0.0
-        ).astype(BF)
+    copies[3].wait()
     zero = jnp.zeros((128, 128), BF)
-    copies[3].wait()
     w2 = w2_ref[...]
     w2 = jnp.concatenate(
         [jnp.concatenate([w2, zero], axis=1), jnp.concatenate([zero, w2], axis=1)], axis=0
@@ -80,7 +91,6 @@
     copies[4].wait()
     x = x_ref[...].reshape(rows, 640)
     valid = (iota((128, 640), 1) // 10).astype(F32) < jnp.concatenate([counts] * 5, axis=1)
-    to_all = ((iota((128, 640), 1) % 10) == iota((128, 640), 0)).astype(BF)
     first = mm(x[:, 0:128], to_all)
     ps[...] = jnp.where(rep(valid, 4), x.astype(F32), first).astype(BF)
     origin = total = square = None
@@ -101,9 +111,6 @@
     shift = total / number
     deviation = jnp.sqrt(jnp.maximum(square / number - shift * shift, 0.01))
     pooled = jnp.concatenate([origin + shift, deviation], axis=1).astype(BF)
-    po = iota((256, 256), 0)
-    pi = iota((256, 256), 1)
-    order = ((po // 16 == pi // 4 % 16) & (po // 4 % 4 == pi // 64) & (po % 4 == pi % 4)).astype(BF)
     for half in range(2):
         part = jnp.concatenate(
             [pooled[d * 128 + half * 64 : d * 128 + half * 64 + 64] for d in range(4)], axis=0
@@ -114,9 +121,9 @@
 def pool_slots(tile, pixels, owner, counts, w_pix1, w_pix2):
     return pl.pallas_call(
         pool_kernel,
-        out_shape=jax.ShapeDtypeStruct((32, 16, 256), BF),
+        out_shape=(jax.ShapeDtypeStruct((32, 16, 256), BF), jax.ShapeDtypeStruct((1,), I32)),
         in_specs=[pl.BlockSpec(memory_space=pltpu.SMEM)] + [pl.BlockSpec(memory_space=pl.ANY)] * 5,
-        out_specs=pl.BlockSpec(memory_space=pltpu.VMEM),
+        out_specs=(pl.BlockSpec(memory_space=pltpu.VMEM), pl.BlockSpec(memory_space=pltpu.SMEM)),
         scratch_shapes=[
             pltpu.VMEM((4, 128, 640), BF),
             pltpu.VMEM((16, 128), I32),
@@ -133,7 +140,7 @@
 
 
 def prepare_kernel(
-    block_ref, scale_ref, after, own_any, cloud_any, gain_any, code_any, we_any,
+    block_ref, scale_ref, own_any, cloud_any, gain_any, code_any, we_any,
     pick_ref, mask_ref, row_ref, code_ref, we_ref, own_ref, cloud_ref, gain_ref, sems,
 ):
     pairs = [
@@ -180,7 +187,7 @@
         copy.wait()
 
 
-def prepare(block, scale, after, owner, cloud, gain, code, w_embed):
+def prepare(block, scale, owner, cloud, gain, code, w_embed):
     return pl.pallas_call(
         prepare_kernel,
         out_shape=(
@@ -191,7 +198,7 @@
             jax.ShapeDtypeStruct((256, 1024), BF),
         ),
         in_specs=[pl.BlockSpec(memory_space=pltpu.SMEM)] * 2
-        + [pl.BlockSpec(memory_space=pl.ANY)] * 6,
+        + [pl.BlockSpec(memory_space=pl.ANY)] * 5,
         out_specs=(pl.BlockSpec(memory_space=pltpu.VMEM),) * 5,
         scratch_shapes=[
             pltpu.VMEM((16, 128), I32),
@@ -202,7 +209,7 @@
         compiler_params=pltpu.CompilerParams(vmem_limit_bytes=48 << 20),
         cost_estimate=pl.CostEstimate(flops=0, bytes_accessed=8 << 20, transcendentals=0),
         name="prepare",
-    )(block, scale, after, owner, cloud, gain, code, w_embed)
+    )(block, scale, owner, cloud, gain, code, w_embed)
 
 
 def pick_kernel(pick_ref, rows_ref, out_ref):
@@ -260,7 +267,8 @@
     ones = jnp.ones((256, 128), BF)
     none = jnp.zeros((256, 128), BF)
     means = []
-    for c in range(4):
+
+    def project(c):
         for copy in chunks[c]:
             copy.wait()
         if c < 3:
@@ -270,10 +278,12 @@
         values = mm(normed, w_ref[c, :, 512:768]).astype(BF)
         q_sum = mm((queries * queries).astype(BF), seg)
         k_sum = mm((keys * keys).astype(BF), seg)
-        queries = (queries * (
-            lax.rsqrt(q_sum + 1e-06) * row_ref[0:1, 256 * c : 256 * c + 256]
-        )).astype(BF)
+        scale = row_ref[0:1, 256 * c : 256 * c + 256]
+        queries = (queries * (lax.rsqrt(q_sum + 1e-06) * scale)).astype(BF)
         keys = (keys * lax.rsqrt(k_sum + 1e-06)).astype(BF)
+        return queries, keys, values
+
+    def mix(queries, keys, values):
         for pair in range(2):
             lanes = slice(128 * pair, 128 * pair + 128)
             q_pair = queries[:, lanes]
@@ -286,6 +296,13 @@
                 both = mm(weights, right)
                 mixed.append(both[:, 0:128] / both[:, 128:256])
             means.append(jnp.mean(jnp.where(left, mixed[0], mixed[1]).reshape(32, 8, 128), axis=0))
+
+    current = project(0)
+    for c in range(1, 4):
+        following = project(c)
+        mix(*current)
+        current = following
+    mix(*current)
     mean = jnp.concatenate(means, axis=1)
     high = mean.astype(BF)
     low = (mean - high.astype(F32)).astype(BF)
@@ -316,17 +333,15 @@
     )(tokens, mask, rows, code, w_embed, w_qkv, w_out)
 
 
-def contrast_kernel(scale_ref, block_ref, all_ref, pos_ref, neg_ref, out_ref):
-    others = all_ref[...].reshape(256, 1024).astype(F32)
-    square = others * others
-    high = square.astype(BF)
-    low = (square - high.astype(F32)).astype(BF)
-    ones = jnp.ones((8, 1024), BF)
-    other_sum = mm_nt(ones, high) + mm_nt(ones, low)
-    mine = all_ref[block_ref[0]]
-    anchors = mine.astype(F32)
-    own_sum = jnp.sum(anchors * anchors, axis=1, keepdims=True)
-    similarity = mm_nt(mine, all_ref[...].reshape(256, 1024))
+def contrast_kernel(scale_ref, block_ref, all_ref, pos_ref, neg_ref, out_ref, products):
+    others = all_ref[...].reshape(256, 1024)
+    products[...] = mm_nt(others, others)
+    same = iota((256, 256), 0) == iota((256, 256), 1)
+    other_sum = jnp.sum(jnp.where(same, products[...], 0.0), axis=0, keepdims=True)
+    mine = pl.multiple_of(block_ref[0] * 8, 8)
+    similarity = products[pl.ds(mine, 8), :]
+    own = iota((8, 256), 1) == iota((8, 256), 0) + mine
+    own_sum = jnp.sum(jnp.where(own, similarity, 0.0), axis=1, keepdims=True)
     similarity = similarity * lax.rsqrt(own_sum + 1e-06) * lax.rsqrt(other_sum + 1e-06)
     logits = similarity * scale_ref[0]
     member = iota((8, 256), 1)
@@ -348,6 +363,7 @@
         out_shape=jax.ShapeDtypeStruct((1, 8), F32),
         in_specs=[pl.BlockSpec(memory_space=pltpu.SMEM)] * 2 + [vmem] * 3,
         out_specs=vmem,
+        scratch_shapes=[pltpu.VMEM((256, 256), F32)],
         compiler_params=pltpu.CompilerParams(vmem_limit_bytes=16 << 20),
         name="contrast",
     )(scale, block, others, pos_ids, neg_ids)
@@ -379,13 +395,13 @@
 ):
     block = lax.axis_index("parcel").reshape(1).astype(I32)
     owner = owner.reshape(16, 128)
-    pooled = pool_slots(
+    pooled, place = pool_slots(
         block, tile_pixels, owner, pix_count.reshape(16, 128), w_pix1, w_pix2
     )
     arrived = lax.all_to_all(pooled, "parcel", split_axis=0, concat_axis=0, tiled=True)
     code = jnp.asarray(date_code(32, 1024))
     pick, mask, rows, code, w_embed = prepare(
-        block, head_scale, pooled, owner, cloud, norm_gain.reshape(8, 128), code, w_embed
+        place, head_scale, owner, cloud, norm_gain.reshape(8, 128), code, w_embed
     )
     moving = pick_rows(pick, arrived)
     tokens = lax.all_to_all(moving, "date", split_axis=0, concat_axis=0, tiled=True)

time: 73.6 us -> 72.5 us (0.985)
  local copies, waits for them, and re-layouts: 5.73 us -> 4.75 us
    unnamed x18 -> x16, local copies, waits for them, and re-layouts: 5.65 us -> 4.67 us
  transfers between devices with their start and end apart: 2 -> 2, of which waited for: 2 -> 2; matrix products, arithmetic and copies ran while one was open for 0% -> 0% of each run, Pallas kernels for 1% -> 2%
where the time goes in v4:
time: 72.5 us; the launch traced here: 72 us
  waiting for transfers between devices  22.6 us (31%)
  Pallas kernels  17.1 us (24%)
  starting transfers between devices  15.8 us (22%)
  blocking collectives  10.4 us (14%)
  local copies, waits for them, and re-layouts  4.75 us (7%)
  between operations  1.37 us (2%)
    all_to_all x1, waiting for transfers between devices, per_device(): lax.all_to_all(copies, 'parcel', split_axis=0, concat_axis=0, tiled=True)  16.7 us
    all_to_all x1, starting transfers between devices, per_device(): lax.all_to_all(pooled, 'parcel', split_axis=0, concat_axis=0, tiled=True)  11.2 us
    all_to_all x1, blocking collectives, per_device(): lax.all_to_all(moving, 'date', split_axis=0, concat_axis=0, tiled=True)  10.4 us
    pallas_call x1, Pallas kernels, pool_slots(): pl.pallas_call(pool_kernel, out_shape=(jax.ShapeDtypeStruct((32, 16, 256)...  7.01 us
    pallas_call x1, Pallas kernels, attend(): pl.pallas_call(attend_kernel, out_shape=(jax.ShapeDtypeStruct((8, 1024),...  6.98 us
    all_to_all x1, waiting for transfers between devices, per_device(): lax.all_to_all(pooled, 'parcel', split_axis=0, concat_axis=0, tiled=True)  5.88 us
    unnamed x16, local copies, waits for them, and re-layouts  4.67 us
    all_to_all x1, starting transfers between devices, per_device(): lax.all_to_all(copies, 'parcel', split_axis=0, concat_axis=0, tiled=True)  4.58 us
  transfers between devices with their start and end apart: 2, of which 2 were waited for; matrix products, arithmetic and copies ran while one was open for 0% of the time, Pallas kernels for 2%

profile of v4, /device:TPU:32, one launch (start us, length us, event | category | flops | bytes accessed | tf_op | source)
XLA Modules:
  0.0 72.0 jit_solution(7826353831575606521)
XLA Ops:
  0.6 7.0 %pool_slots.1 = (bf16[32,16,256]{2,1,0:T(8,128)(2,1)}, s32[1]{0:T(128)}) custom-call(s32[1]{0:T(128)} %bitcast.tile_ref.block_ref, bf16[4,128,640]{2,1,0:T(8,128)(2,1)} %x_any.1, s32[16,128]{1,0:T(8,128)} %bitcast.8, s32[16,128]{1,0:T(8,128)} %bitcast.11, bf16[10,128]{1,0:T(8,128)(2,1)} %w1_any.1, bf16[128,128]{1,0:T(8,128)(2,1)} %w2_any.1), custom_call_target="tpu_custom_call" | custom-call | tf_op jit(solution)/shard_map/pool_slots/pallas_call | solution.py:122
  7.6 0.0 copy-start.7
  7.7 0.0 copy-start.4
  7.7 11.2 %all-to-all-start = ((bf16[32,16,256]{2,1,0:T(8,128)(2,1)}), bf16[32,16,256]{2,1,0:T(8,128)(2,1)S(1)}, u32[]{:S(2)}, u32[]{:S(2)}) async-start(bf16[32,16,256]{2,1,0:T(8,128)(2,1)} %get-tuple-element.13), calls=%async_computation | async-start | bytes 524288 | tf_op jit(solution)/shard_map/all_to_all | solution.py:401
  18.9 0.0 copy-start
  18.9 1.0 %copy-done = bf16[256,1024]{1,0:T(8,128)(2,1)S(1)} copy-done((bf16[256,1024]{1,0:T(8,128)(2,1)S(1)}, bf16[256,1024]{1,0:T(8,128)(2,1)}, u32[]{:S(2)}) %copy-start) | copy-done | bytes 524312
  19.9 0.0 copy-start.1
  19.9 0.9 %copy-done.1 = f32[32,1024]{1,0:T(8,128)S(1)} copy-done((f32[32,1024]{1,0:T(8,128)S(1)}, f32[32,1024]{1,0:T(8,128)}, u32[]{:S(2)}) %copy-start.1) | copy-done | bytes 131096
  20.8 0.0 copy-start.2
  20.8 0.7 copy-done.2
  21.5 0.0 copy-start.3
  21.5 0.7 copy-done.3
  22.2 0.0 copy-start.5
  22.2 0.7 copy-done.5
  22.9 0.0 copy-start.6
  22.9 0.7 copy-done.6
  23.6 1.7 %prepare.1 = (bf16[256,512]{1,0:T(8,128)(2,1)S(1)}, f32[256,256]{1,0:T(8,128)S(1)}, f32[8,1024]{1,0:T(8,128)S(1)}, f32[32,1024]{1,0:T(8,128)S(1)}, bf16[256,1024]{1,0:T(8,128)(2,1)S(1)}) custom-call(s32[1]{0:T(128)} %get-tuple-element.11.block_ref, f32[16]{0:T(128)S(1)} %copy-done.6, s32[16,128]{1,0:T(8,128)S(1)} %bitcast.9, s32[8,32]{1,0:T(8,128)S(1)} %copy-done.3, ...), custom_call_target="tpu_custom_call" | custom-call | bytes 8388608 | tf_op jit(solution)/shard_map/prepare/pallas_call | solution.py:191
  25.3 5.9 %all-to-all-done.rows_ref = bf16[32,16,256]{2,1,0:T(8,128)(2,1)S(1)} async-done(((bf16[32,16,256]{2,1,0:T(8,128)(2,1)}), bf16[32,16,256]{2,1,0:T(8,128)(2,1)S(1)}, u32[]{:S(2)}, u32[]{:S(2)}) %all-to-all-start) | async-done | bytes 262176 | tf_op jit(solution)/shard_map/all_to_all | solution.py:401
  31.2 0.2 pick_rows.1
  31.4 10.4 %all_to_all.15 = bf16[8,32,256]{2,1,0:T(8,128)(2,1)S(1)} all-to-all(bf16[8,32,256]{2,1,0:T(8,128)(2,1)S(1)} %pick_rows.1), channel_id=1, replica_groups=mesh['date'=8,'parcel'=32] {'date'}, dimensions={0} | all-to-all | bytes 262144 | tf_op jit(solution)/shard_map/all_to_all | solution.py:407
  41.8 7.0 %attend.1 = (bf16[8,1024]{1,0:T(8,128)(2,1)}, bf16[32,8,1024]{2,1,0:T(8,128)(2,1)}) custom-call(bf16[256,256]{1,0:T(8,128)(2,1)S(1)} %bitcast.7, f32[256,256]{1,0:T(8,128)S(1)} %get-tuple-element.14.mask_ref, f32[8,1024]{1,0:T(8,128)S(1)} %get-tuple-element.15.row_ref, f32[32,1024]{1,0:T(8,128)S(1)} %get-tuple-element.16.code_ref, ...), custom_call_target="tpu_custom_call" | custom-call | tf_op jit(solution)/shard_map/attend/pallas_call | solution.py:318
  48.8 4.6 %all-to-all-start.2 = ((bf16[32,8,1024]{2,1,0:T(8,128)(2,1)}), bf16[32,8,1024]{2,1,0:T(8,128)(2,1)S(1)}, u32[]{:S(2)}, u32[]{:S(2)}) async-start(bf16[32,8,1024]{2,1,0:T(8,128)(2,1)} %get-tuple-element.19), calls=%async_computation.2 | async-start | bytes 1048576 | tf_op jit(solution)/shard_map/all_to_all | solution.py:417
  54.0 0.0 copy-done.7
  54.0 0.1 copy.17.pos_ref
  54.1 16.7 %all-to-all-done.2.all_ref = bf16[32,8,1024]{2,1,0:T(8,128)(2,1)S(1)} async-done(((bf16[32,8,1024]{2,1,0:T(8,128)(2,1)}), bf16[32,8,1024]{2,1,0:T(8,128)(2,1)S(1)}, u32[]{:S(2)}, u32[]{:S(2)}) %all-to-all-start.2) | async-done | bytes 524320 | tf_op jit(solution)/shard_map/all_to_all | solution.py:417
  70.8 0.0 copy-done.4
  70.8 1.1 %contrast.1 = f32[1,8]{1,0:T(1,128)} custom-call(f32[1]{0:T(128)S(6)} %copy.18.scale_ref, s32[1]{0:T(128)} %bitcast.tile_ref.block_ref, bf16[32,8,1024]{2,1,0:T(8,128)(2,1)S(1)} %all-to-all-done.2.all_ref, s32[8,1]{1,0:T(8,128)S(1)} %copy.17.pos_ref, s32[8,128]{1,0:T(8,128)S(1)} %copy-done.4), custom_call_target="tpu_custom_call" | custom-call | tf_op jit(solution)/shard_map/contrast/pallas_call | solution.py:361
Async XLA Ops:
  7.6 46.4 %copy-start.7 = (s32[8]{0:T(128)S(1)}, s32[8]{0:T(128)}, u32[]{:S(2)}) copy-start(s32[8]{0:T(128)} %param.27) | copy-start | bytes 100
  7.7 63.2 %copy-start.4 = (s32[8,128]{1,0:T(8,128)S(1)}, s32[8,128]{1,0:T(8,128)}, u32[]{:S(2)}) copy-start(s32[8,128]{1,0:T(8,128)} %neg_ref.1) | copy-start | bytes 12292
  7.7 23.5 %all-to-all-start = ((bf16[32,16,256]{2,1,0:T(8,128)(2,1)}), bf16[32,16,256]{2,1,0:T(8,128)(2,1)S(1)}, u32[]{:S(2)}, u32[]{:S(2)}) async-start(bf16[32,16,256]{2,1,0:T(8,128)(2,1)} %get-tuple-element.13), calls=%async_computation | async-start | bytes 524288 | tf_op jit(solution)/shard_map/all_to_all | solution.py:401
  18.9 1.0 %copy-start = (bf16[256,1024]{1,0:T(8,128)(2,1)S(1)}, bf16[256,1024]{1,0:T(8,128)(2,1)}, u32[]{:S(2)}) copy-start(bf16[256,1024]{1,0:T(8,128)(2,1)} %we_any.1) | copy-start | bytes 1572868
  19.9 0.9 %copy-start.1 = (f32[32,1024]{1,0:T(8,128)S(1)}, f32[32,1024]{1,0:T(8,128)}, u32[]{:S(2)}) copy-start(f32[32,1024]{1,0:T(8,128)} %constant.6.clone.code_any) | copy-start | bytes 393220
  20.8 0.7 copy-start.2
  21.5 0.7 copy-start.3
  22.2 0.7 copy-start.5
  22.9 0.7 copy-start.6
  48.8 22.0 %all-to-all-start.2 = ((bf16[32,8,1024]{2,1,0:T(8,128)(2,1)}), bf16[32,8,1024]{2,1,0:T(8,128)(2,1)S(1)}, u32[]{:S(2)}, u32[]{:S(2)}) async-start(bf16[32,8,1024]{2,1,0:T(8,128)(2,1)} %get-tuple-element.19), calls=%async_computation.2 | async-start | bytes 1048576 | tf_op jit(solution)/shard_map/all_to_all | solution.py:417

commit v5 on v4

--- a/solution.py
+++ b/solution.py
@@ -233,28 +233,19 @@
     tok_ref, mask_ref, row_ref, code_ref, we_ref, wqkv_any, wo_any,
     emb_ref, all_ref, w_ref, wo_ref, sems,
 ):
-    chunks = [
-        [
+    for c in range(4):
+        for part in range(3):
+            columns = pl.ds(1024 * part + 256 * c, 256)
             pltpu.make_async_copy(
-                wqkv_any.at[:, 1024 * part + 256 * c : 1024 * part + 256 * c + 256],
+                wqkv_any.at[:, columns],
                 w_ref.at[c, :, 256 * part : 256 * part + 256],
-                sems.at[3 * c + part],
-            )
-            for part in range(3)
-        ]
-        for c in range(4)
-    ]
-    chunks.append([pltpu.make_async_copy(wo_any, wo_ref, sems.at[12])])
-
-    def start(number):
-        for copy in chunks[number]:
-            copy.start()
-
-    start(0)
+                sems.at[c],
+            ).start()
+    last = pltpu.make_async_copy(wo_any, wo_ref, sems.at[4])
+    last.start()
     encoded = mm(tok_ref[...], we_ref[...]).astype(BF).astype(F32)
     code = jnp.broadcast_to(code_ref[...][:, None, :], (32, 8, 1024)).reshape(256, 1024)
     state = encoded + code
-    start(1)
     state_mean = jnp.mean(state.reshape(32, 8, 1024), axis=0)
     center = jnp.mean(state, axis=1, keepdims=True)
     moved = state - center
@@ -269,10 +260,8 @@
     means = []
 
     def project(c):
-        for copy in chunks[c]:
-            copy.wait()
-        if c < 3:
-            start(c + 2)
+        for part in ((0,), (1,), (2, 3), ())[c]:
+            pltpu.make_async_copy(w_ref.at[part], w_ref.at[part], sems.at[part]).wait()
         queries = mm(normed, w_ref[c, :, 0:256])
         keys = mm(normed, w_ref[c, :, 256:512])
         values = mm(normed, w_ref[c, :, 512:768]).astype(BF)
@@ -306,7 +295,7 @@
     mean = jnp.concatenate(means, axis=1)
     high = mean.astype(BF)
     low = (mean - high.astype(F32)).astype(BF)
-    chunks[4][0].wait()
+    last.wait()
     update = mm(jnp.concatenate([high, low], axis=0), wo_ref[...])
     embedding = (state_mean + (update[0:8] + update[8:16])).astype(BF)
     emb_ref[...] = embedding
@@ -326,7 +315,7 @@
         scratch_shapes=[
             pltpu.VMEM((4, 1024, 768), BF),
             pltpu.VMEM((1024, 1024), BF),
-            pltpu.SemaphoreType.DMA((13,)),
+            pltpu.SemaphoreType.DMA((5,)),
         ],
         compiler_params=pltpu.CompilerParams(vmem_limit_bytes=52 << 20),
         name="attend",

time: 72.5 us -> 72.2 us (level)
  no operation moved by 1% of the time
where the time goes in v5:
time: 72.2 us; the launch traced here: 71.6 us
  waiting for transfers between devices  22.6 us (31%)
  Pallas kernels  16.7 us (23%)
  starting transfers between devices  15.8 us (22%)
  blocking collectives  10.4 us (14%)
  local copies, waits for them, and re-layouts  4.75 us (7%)
  between operations  1.37 us (2%)
    all_to_all x1, waiting for transfers between devices, per_device(): lax.all_to_all(copies, 'parcel', split_axis=0, concat_axis=0, tiled=True)  16.7 us
    all_to_all x1, starting transfers between devices, per_device(): lax.all_to_all(pooled, 'parcel', split_axis=0, concat_axis=0, tiled=True)  11.2 us
    all_to_all x1, blocking collectives, per_device(): lax.all_to_all(moving, 'date', split_axis=0, concat_axis=0, tiled=True)  10.4 us
    pallas_call x1, Pallas kernels, pool_slots(): pl.pallas_call(pool_kernel, out_shape=(jax.ShapeDtypeStruct((32, 16, 256)...  7.01 us
    pallas_call x1, Pallas kernels, attend(): pl.pallas_call(attend_kernel, out_shape=(jax.ShapeDtypeStruct((8, 1024),...  6.64 us
    all_to_all x1, waiting for transfers between devices, per_device(): lax.all_to_all(pooled, 'parcel', split_axis=0, concat_axis=0, tiled=True)  5.88 us
    unnamed x16, local copies, waits for them, and re-layouts  4.67 us
    all_to_all x1, starting transfers between devices, per_device(): lax.all_to_all(copies, 'parcel', split_axis=0, concat_axis=0, tiled=True)  4.58 us
  transfers between devices with their start and end apart: 2, of which 2 were waited for; matrix products, arithmetic and copies ran while one was open for 0% of the time, Pallas kernels for 2%

profile of v5, /device:TPU:32, one launch (start us, length us, event | category | flops | bytes accessed | tf_op | source)
XLA Modules:
  0.0 71.6 jit_solution(4726728204630276966)
XLA Ops:
  0.6 7.0 %pool_slots.1 = (bf16[32,16,256]{2,1,0:T(8,128)(2,1)}, s32[1]{0:T(128)}) custom-call(s32[1]{0:T(128)} %bitcast.tile_ref.block_ref, bf16[4,128,640]{2,1,0:T(8,128)(2,1)} %x_any.1, s32[16,128]{1,0:T(8,128)} %bitcast.8, s32[16,128]{1,0:T(8,128)} %bitcast.11, bf16[10,128]{1,0:T(8,128)(2,1)} %w1_any.1, bf16[128,128]{1,0:T(8,128)(2,1)} %w2_any.1), custom_call_target="tpu_custom_call" | custom-call | tf_op jit(solution)/shard_map/pool_slots/pallas_call | solution.py:122
  7.6 0.0 copy-start.7
  7.7 0.0 copy-start.4
  7.7 11.2 %all-to-all-start = ((bf16[32,16,256]{2,1,0:T(8,128)(2,1)}), bf16[32,16,256]{2,1,0:T(8,128)(2,1)S(1)}, u32[]{:S(2)}, u32[]{:S(2)}) async-start(bf16[32,16,256]{2,1,0:T(8,128)(2,1)} %get-tuple-element.13), calls=%async_computation | async-start | bytes 524288 | tf_op jit(solution)/shard_map/all_to_all | solution.py:390
  18.9 0.0 copy-start
  18.9 1.0 %copy-done = bf16[256,1024]{1,0:T(8,128)(2,1)S(1)} copy-done((bf16[256,1024]{1,0:T(8,128)(2,1)S(1)}, bf16[256,1024]{1,0:T(8,128)(2,1)}, u32[]{:S(2)}) %copy-start) | copy-done | bytes 524312
  19.9 0.0 copy-start.1
  19.9 0.9 %copy-done.1 = f32[32,1024]{1,0:T(8,128)S(1)} copy-done((f32[32,1024]{1,0:T(8,128)S(1)}, f32[32,1024]{1,0:T(8,128)}, u32[]{:S(2)}) %copy-start.1) | copy-done | bytes 131096
  20.8 0.0 copy-start.2
  20.8 0.7 copy-done.2
  21.5 0.0 copy-start.3
  21.5 0.7 copy-done.3
  22.2 0.0 copy-start.5
  22.2 0.7 copy-done.5
  22.9 0.0 copy-start.6
  22.9 0.7 copy-done.6
  23.6 1.7 %prepare.1 = (bf16[256,512]{1,0:T(8,128)(2,1)S(1)}, f32[256,256]{1,0:T(8,128)S(1)}, f32[8,1024]{1,0:T(8,128)S(1)}, f32[32,1024]{1,0:T(8,128)S(1)}, bf16[256,1024]{1,0:T(8,128)(2,1)S(1)}) custom-call(s32[1]{0:T(128)} %get-tuple-element.11.block_ref, f32[16]{0:T(128)S(1)} %copy-done.6, s32[16,128]{1,0:T(8,128)S(1)} %bitcast.9, s32[8,32]{1,0:T(8,128)S(1)} %copy-done.3, ...), custom_call_target="tpu_custom_call" | custom-call | bytes 8388608 | tf_op jit(solution)/shard_map/prepare/pallas_call | solution.py:191
  25.3 5.9 %all-to-all-done.rows_ref = bf16[32,16,256]{2,1,0:T(8,128)(2,1)S(1)} async-done(((bf16[32,16,256]{2,1,0:T(8,128)(2,1)}), bf16[32,16,256]{2,1,0:T(8,128)(2,1)S(1)}, u32[]{:S(2)}, u32[]{:S(2)}) %all-to-all-start) | async-done | bytes 262176 | tf_op jit(solution)/shard_map/all_to_all | solution.py:390
  31.2 0.2 pick_rows.1
  31.4 10.4 %all_to_all.15 = bf16[8,32,256]{2,1,0:T(8,128)(2,1)S(1)} all-to-all(bf16[8,32,256]{2,1,0:T(8,128)(2,1)S(1)} %pick_rows.1), channel_id=1, replica_groups=mesh['date'=8,'parcel'=32] {'date'}, dimensions={0} | all-to-all | bytes 262144 | tf_op jit(solution)/shard_map/all_to_all | solution.py:396
  41.8 6.6 %attend.1 = (bf16[8,1024]{1,0:T(8,128)(2,1)}, bf16[32,8,1024]{2,1,0:T(8,128)(2,1)}) custom-call(bf16[256,256]{1,0:T(8,128)(2,1)S(1)} %bitcast.7, f32[256,256]{1,0:T(8,128)S(1)} %get-tuple-element.14.mask_ref, f32[8,1024]{1,0:T(8,128)S(1)} %get-tuple-element.15.row_ref, f32[32,1024]{1,0:T(8,128)S(1)} %get-tuple-element.16.code_ref, ...), custom_call_target="tpu_custom_call" | custom-call | tf_op jit(solution)/shard_map/attend/pallas_call | solution.py:307
  48.5 4.6 %all-to-all-start.2 = ((bf16[32,8,1024]{2,1,0:T(8,128)(2,1)}), bf16[32,8,1024]{2,1,0:T(8,128)(2,1)S(1)}, u32[]{:S(2)}, u32[]{:S(2)}) async-start(bf16[32,8,1024]{2,1,0:T(8,128)(2,1)} %get-tuple-element.19), calls=%async_computation.2 | async-start | bytes 1048576 | tf_op jit(solution)/shard_map/all_to_all | solution.py:406
  53.7 0.0 copy-done.7
  53.7 0.1 copy.17.pos_ref
  53.8 16.7 %all-to-all-done.2.all_ref = bf16[32,8,1024]{2,1,0:T(8,128)(2,1)S(1)} async-done(((bf16[32,8,1024]{2,1,0:T(8,128)(2,1)}), bf16[32,8,1024]{2,1,0:T(8,128)(2,1)S(1)}, u32[]{:S(2)}, u32[]{:S(2)}) %all-to-all-start.2) | async-done | bytes 524320 | tf_op jit(solution)/shard_map/all_to_all | solution.py:406
  70.5 0.0 copy-done.4
  70.5 1.1 %contrast.1 = f32[1,8]{1,0:T(1,128)} custom-call(f32[1]{0:T(128)S(6)} %copy.18.scale_ref, s32[1]{0:T(128)} %bitcast.tile_ref.block_ref, bf16[32,8,1024]{2,1,0:T(8,128)(2,1)S(1)} %all-to-all-done.2.all_ref, s32[8,1]{1,0:T(8,128)S(1)} %copy.17.pos_ref, s32[8,128]{1,0:T(8,128)S(1)} %copy-done.4), custom_call_target="tpu_custom_call" | custom-call | tf_op jit(solution)/shard_map/contrast/pallas_call | solution.py:350
Async XLA Ops:
  7.6 46.0 %copy-start.7 = (s32[8]{0:T(128)S(1)}, s32[8]{0:T(128)}, u32[]{:S(2)}) copy-start(s32[8]{0:T(128)} %param.27) | copy-start | bytes 100
  7.7 62.8 %copy-start.4 = (s32[8,128]{1,0:T(8,128)S(1)}, s32[8,128]{1,0:T(8,128)}, u32[]{:S(2)}) copy-start(s32[8,128]{1,0:T(8,128)} %neg_ref.1) | copy-start | bytes 12292
  7.7 23.5 %all-to-all-start = ((bf16[32,16,256]{2,1,0:T(8,128)(2,1)}), bf16[32,16,256]{2,1,0:T(8,128)(2,1)S(1)}, u32[]{:S(2)}, u32[]{:S(2)}) async-start(bf16[32,16,256]{2,1,0:T(8,128)(2,1)} %get-tuple-element.13), calls=%async_computation | async-start | bytes 524288 | tf_op jit(solution)/shard_map/all_to_all | solution.py:390
  18.9 1.0 %copy-start = (bf16[256,1024]{1,0:T(8,128)(2,1)S(1)}, bf16[256,1024]{1,0:T(8,128)(2,1)}, u32[]{:S(2)}) copy-start(bf16[256,1024]{1,0:T(8,128)(2,1)} %we_any.1) | copy-start | bytes 1572868
  19.9 0.9 %copy-start.1 = (f32[32,1024]{1,0:T(8,128)S(1)}, f32[32,1024]{1,0:T(8,128)}, u32[]{:S(2)}) copy-start(f32[32,1024]{1,0:T(8,128)} %constant.6.clone.code_any) | copy-start | bytes 393220
  20.8 0.7 copy-start.2
  21.5 0.7 copy-start.3
  22.2 0.7 copy-start.5
  22.9 0.7 copy-start.6
  48.5 22.0 %all-to-all-start.2 = ((bf16[32,8,1024]{2,1,0:T(8,128)(2,1)}), bf16[32,8,1024]{2,1,0:T(8,128)(2,1)S(1)}, u32[]{:S(2)}, u32[]{:S(2)}) async-start(bf16[32,8,1024]{2,1,0:T(8,128)(2,1)} %get-tuple-element.19), calls=%async_computation.2 | async-start | bytes 1048576 | tf_op jit(solution)/shard_map/all_to_all | solution.py:406
